TPU v7x, 128 devices: a whole 4x4x4 slice. The times are simulated.
128 devices in a mesh: row: 8 (over x_lo, z), col: 16 (over y, x_hi, core).
Axes of the slice: x: 4 (x_hi: 2, x_lo: 2; x = x_hi * 2 + x_lo), y: 4, z: 4, core: 2. Of those that a mesh axis runs over, the one named last changes fastest.
Arguments:
- unfolding: bfloat16 [6144, 4096], P('row', 'col'), may hold values from -400 to 400
Outputs:
- regrouped: bfloat16 [256, 16, 6144], P('col', None, 'row')
All inputs are finite; a program needn't handle non-finite values.
Results may differ from a plain program's by a relative error of at most 0.0062.
Values may be sent and summed in bfloat16 or wider, within the bound.
No kernel may reach another device: no remote copies, remote signals or barrier semaphores. Data moves between devices by JAX's collectives and lax.ppermute only.
A program may use at most 64 MiB of HBM per device.

v0:
```python
import math

import jax
import jax.numpy as jnp
from jax import lax
from jax.sharding import PartitionSpec as P

PIXELS = 256
ITERS = 2
COLS = 4096


def local(unfolding):
    rows_dev = unfolding.shape[0]
    cols_dev = unfolding.shape[1]
    total_rows = rows_dev * lax.axis_size("row")
    values = unfolding.astype(jnp.float32)
    sumsq = lax.psum(jnp.sum(values * values), ("row", "col"))
    factor = math.sqrt(COLS) / (3.0 * jnp.sqrt(sumsq))
    current = (values * factor).astype(jnp.bfloat16)
    updated = current.astype(jnp.float32)
    for turn_index in range(ITERS):
        gathered = lax.all_gather(current, "col", axis=1, tiled=True)
        partial_gram = lax.dot_general(
            current, gathered, (((0,), (0,)), ((), ())), preferred_element_type=jnp.float32
        )
        shares = lax.psum_scatter(partial_gram, "row", scatter_dimension=1, tiled=True).astype(
            jnp.bfloat16
        )
        gram_rows = lax.all_gather(shares, "row", axis=1, tiled=True)
        first = lax.dot_general(
            gathered, gram_rows, (((1,), (1,)), ((), ())), preferred_element_type=jnp.float32
        ).astype(jnp.bfloat16)
        second = lax.dot_general(
            lax.all_gather(first, "col", axis=1, tiled=True),
            gram_rows,
            (((1,), (1,)), ((), ())),
            preferred_element_type=jnp.float32,
        )
        updated = (
            1.875 * current.astype(jnp.float32) - 1.25 * first.astype(jnp.float32) + 0.375 * second
        )
        if turn_index + 1 < ITERS:
            current = updated.astype(jnp.bfloat16)
    final = updated * math.sqrt(total_rows)
    view_count = cols_dev // PIXELS
    cube = final.reshape(rows_dev, view_count, PIXELS).transpose(2, 1, 0).astype(jnp.bfloat16)
    return lax.all_to_all(cube, "col", split_axis=0, concat_axis=1, tiled=True)


def solution(mesh):
    return jax.shard_map(
        local,
        mesh=mesh,
        in_specs=(P("row", "col"),),
        out_specs=P("col", None, "row"),
        check_vma=False,
    )
```

profile of v0, /device:TPU:1, one launch (start us, length us, event | category | flops | bytes accessed | tf_op | source)
XLA Modules:
  0.0 585.2 jit_solution(2471364710384722824)
XLA Ops:
  6.5 0.0 all-gather.7.cloned.1.call-start
  6.5 1.8 fusion.6
  8.3 68.7 %psum.7 = f32[]{:T(128)} all-reduce(f32[]{:T(128)} %fusion.6), channel_id=1, replica_groups=mesh['row'=8,'col'=16] {'row','col'}, use_global_device_ids=true, to_apply=%region_1.0 | all-reduce | flops 1 | bytes 8 | tf_op jit(solution)/shard_map/psum | solution.py:18
  77.7 1.8 fusion.7
  79.6 0.0 all-gather.7.cloned.1.call-update
  79.6 0.0 reduce-scatter.3.cloned.1.call-start
  79.6 63.6 %all-gather.7.cloned.1.call-done = bf16[768,4096]{1,0:T(8,128)(2,1)} async-done(((bf16[768,256]{1,0:T(8,128)(2,1)}), bf16[768,4096]{1,0:T(8,128)(2,1)}) %all-gather.7.cloned.1.call-update) | async-done | bytes 6291472 | tf_op jit(solution)/shard_map/all_gather | solution.py:23
  143.2 6.8 %fusion.8 = f32[256,4096]{1,0:T(8,128)} fusion(bf16[768,256]{1,0:T(8,128)(2,1)} %fusion.7, bf16[768,4096]{1,0:T(8,128)(2,1)} %all-gather.7.cloned.1.call-done), kind=kOutput, calls=%fused_computation.14 | convolution fusion | flops 1610612736 | bytes 10878976 | tf_op jit(solution)/shard_map/dot_general | solution.py:24
  150.0 0.0 reduce-scatter.3.cloned.1.call-update
  150.0 0.0 all-gather.9.cloned.1.call-start
  150.1 50.7 %reduce-scatter.3.cloned.1.call-done = f32[256,512]{1,0:T(8,128)} async-done(((f32[256,4096]{1,0:T(8,128)}), f32[256,512]{1,0:T(8,128)}) %reduce-scatter.3.cloned.1.call-update) | async-done | bytes 524304 | tf_op jit(solution)/shard_map/reduce_scatter | solution.py:27
  200.8 1.8 convert_element_type.45
  202.6 0.0 copy-start
  202.6 0.0 all-gather.9.cloned.1.call-update
  202.6 0.0 all-gather.11.cloned.1.call-start
  202.7 35.1 %all-gather.9.cloned.1.call-done = bf16[256,4096]{1,0:T(8,128)(2,1)} async-done(((bf16[256,512]{1,0:T(8,128)(2,1)}), bf16[256,4096]{1,0:T(8,128)(2,1)}) %all-gather.9.cloned.1.call-update) | async-done | bytes 2097168 | tf_op jit(solution)/shard_map/all_gather | solution.py:30
  237.8 0.0 copy-start.2
  237.8 6.1 %convolution_convert_fusion.1 = bf16[768,256]{1,0:T(8,128)(2,1)} fusion(bf16[768,4096]{1,0:T(8,128)(2,1)} %all-gather.7.cloned.1.call-done, bf16[256,4096]{1,0:T(8,128)(2,1)} %all-gather.9.cloned.1.call-done), kind=kOutput, calls=%fused_computation.8 | convolution fusion | flops 1610809344 | bytes 8781824 | tf_op jit(solution)/shard_map/dot_general | solution.py:31
  243.9 0.0 all-gather.11.cloned.1.call-update
  244.0 0.0 all-gather.13.cloned.1.call-start
  244.0 71.6 %all-gather.11.cloned.1.call-done = bf16[768,4096]{1,0:T(8,128)(2,1)} async-done(((bf16[768,256]{1,0:T(8,128)(2,1)}), bf16[768,4096]{1,0:T(8,128)(2,1)}) %all-gather.11.cloned.1.call-update) | async-done | bytes 6291472 | tf_op jit(solution)/shard_map/all_gather | solution.py:35
  315.6 0.0 copy-done
  315.6 0.0 copy-done.2
  315.6 5.4 fusion.3
  321.0 0.0 all-gather.13.cloned.1.call-update
  321.1 0.0 reduce-scatter.5.cloned.1.call-start
  321.1 64.4 %all-gather.13.cloned.1.call-done = bf16[768,4096]{1,0:T(8,128)(2,1)} async-done(((bf16[768,256]{1,0:T(8,128)(2,1)}), bf16[768,4096]{1,0:T(8,128)(2,1)}) %all-gather.13.cloned.1.call-update) | async-done | bytes 6291472 | tf_op jit(solution)/shard_map/all_gather | solution.py:23
  385.5 6.8 %fusion.9 = f32[256,4096]{1,0:T(8,128)} fusion(bf16[768,256]{1,0:T(8,128)(2,1)} %fusion.3, bf16[768,4096]{1,0:T(8,128)(2,1)} %all-gather.13.cloned.1.call-done), kind=kOutput, calls=%fused_computation.15 | convolution fusion | flops 1610612736 | bytes 10878976 | tf_op jit(solution)/shard_map/dot_general | solution.py:24
  392.3 0.0 reduce-scatter.5.cloned.1.call-update
  392.4 0.0 all-gather.15.cloned.1.call-start
  392.4 50.7 %reduce-scatter.5.cloned.1.call-done = f32[256,512]{1,0:T(8,128)} async-done(((f32[256,4096]{1,0:T(8,128)}), f32[256,512]{1,0:T(8,128)}) %reduce-scatter.5.cloned.1.call-update) | async-done | bytes 524304 | tf_op jit(solution)/shard_map/reduce_scatter | solution.py:27
  443.1 1.8 convert_element_type.50
  444.9 0.0 copy-start.1
  444.9 0.0 all-gather.15.cloned.1.call-update
  444.9 0.2 all-gather.17.cloned.1.call-start
  445.2 35.0 %all-gather.15.cloned.1.call-done = bf16[256,4096]{1,0:T(8,128)(2,1)} async-done(((bf16[256,512]{1,0:T(8,128)(2,1)}), bf16[256,4096]{1,0:T(8,128)(2,1)}) %all-gather.15.cloned.1.call-update) | async-done | bytes 2097168 | tf_op jit(solution)/shard_map/all_gather | solution.py:30
  480.1 0.0 copy-start.3
  480.1 6.1 %convolution_convert_fusion = bf16[768,256]{1,0:T(8,128)(2,1)} fusion(bf16[768,4096]{1,0:T(8,128)(2,1)} %all-gather.13.cloned.1.call-done, bf16[256,4096]{1,0:T(8,128)(2,1)} %all-gather.15.cloned.1.call-done), kind=kOutput, calls=%fused_computation.7 | convolution fusion | flops 1610809344 | bytes 8781824 | tf_op jit(solution)/shard_map/dot_general | solution.py:31
  486.3 0.0 all-gather.17.cloned.1.call-update
  486.3 71.7 %all-gather.17.cloned.1.call-done = bf16[768,4096]{1,0:T(8,128)(2,1)} async-done(((bf16[768,256]{1,0:T(8,128)(2,1)}), bf16[768,4096]{1,0:T(8,128)(2,1)}) %all-gather.17.cloned.1.call-update) | async-done | bytes 6291472 | tf_op jit(solution)/shard_map/all_gather | solution.py:35
  558.0 0.0 copy-done.1
  558.0 0.0 copy-done.3
  558.0 4.7 fusion.5
  562.6 0.5 broadcast.18
  563.2 0.9 reduce
  564.1 0.2 copy.8
  564.3 0.1 reshape.2
  564.4 12.7 %all_to_all.18 = bf16[16,2,6144]{2,1,0:T(2,128)(2,1)S(1)} all-to-all(bf16[16,2,6144]{2,1,0:T(2,128)(2,1)S(1)} %reshape.2), channel_id=1, replica_groups=mesh['row'=8,'col'=16] {'col'}, dimensions={0} | all-to-all | bytes 786432 | tf_op jit(solution)/shard_map/all_to_all | solution.py:48
  577.0 0.4 reshape.3
  577.5 0.9 copy.6
  (1 shorter events, 0.0 us)
Async XLA Ops:
  6.5 136.7 %all-gather.7.cloned.1.call-start = ((), (), s32[]{:S(2)}) async-start(), calls=%async_computation.3 | async-start | bytes 6684672 | tf_op jit(solution)/shard_map/all_gather | solution.py:23
  79.6 121.2 %reduce-scatter.3.cloned.1.call-start = ((), (), s32[]{:S(2)}) async-start(), calls=%async_computation.4 | async-start | bytes 4718592 | tf_op jit(solution)/shard_map/reduce_scatter | solution.py:27
  150.0 87.8 %all-gather.9.cloned.1.call-start = ((), (), s32[]{:S(2)}) async-start(), calls=%async_computation.5 | async-start | bytes 2359296 | tf_op jit(solution)/shard_map/all_gather | solution.py:30
  202.6 113.1 %copy-start = (bf16[768,256]{1,0:T(8,128)(2,1)S(1)}, bf16[768,256]{1,0:T(8,128)(2,1)}, u32[]{:S(2)}) copy-start(bf16[768,256]{1,0:T(8,128)(2,1)} %fusion.7) | copy-start | bytes 1179652
  202.6 113.0 %all-gather.11.cloned.1.call-start = ((), (), s32[]{:S(2)}) async-start(), calls=%async_computation.6 | async-start | bytes 6684672 | tf_op jit(solution)/shard_map/all_gather | solution.py:35
  237.8 77.8 %copy-start.2 = (bf16[256,4096]{1,0:T(8,128)(2,1)S(1)}, bf16[256,4096]{1,0:T(8,128)(2,1)}, u32[]{:S(2)}) copy-start(bf16[256,4096]{1,0:T(8,128)(2,1)} %all-gather.9.cloned.1.call-done) | copy-start | bytes 6291460
  244.0 141.6 %all-gather.13.cloned.1.call-start = ((), (), s32[]{:S(2)}) async-start(), calls=%async_computation.7 | async-start | bytes 6684672 | tf_op jit(solution)/shard_map/all_gather | solution.py:23
  321.1 122.0 %reduce-scatter.5.cloned.1.call-start = ((), (), s32[]{:S(2)}) async-start(), calls=%async_computation.8 | async-start | bytes 4718592 | tf_op jit(solution)/shard_map/reduce_scatter | solution.py:27
  392.4 87.8 %all-gather.15.cloned.1.call-start = ((), (), s32[]{:S(2)}) async-start(), calls=%async_computation.9 | async-start | bytes 2359296 | tf_op jit(solution)/shard_map/all_gather | solution.py:30
  444.9 113.0 %copy-start.1 = (bf16[768,256]{1,0:T(8,128)(2,1)S(1)}, bf16[768,256]{1,0:T(8,128)(2,1)}, u32[]{:S(2)}) copy-start(bf16[768,256]{1,0:T(8,128)(2,1)} %fusion.3) | copy-start | bytes 1179652
  444.9 113.0 %all-gather.17.cloned.1.call-start = ((), (), s32[]{:S(2)}) async-start(), calls=%async_computation.10 | async-start | bytes 6684672 | tf_op jit(solution)/shard_map/all_gather | solution.py:35
  480.1 77.8 %copy-start.3 = (bf16[256,4096]{1,0:T(8,128)(2,1)S(1)}, bf16[256,4096]{1,0:T(8,128)(2,1)}, u32[]{:S(2)}) copy-start(bf16[256,4096]{1,0:T(8,128)(2,1)} %all-gather.15.cloned.1.call-done) | copy-start | bytes 6291460
Sparse Core Ops, SparseCore 0:
  79.7 63.4 all-gather.6
  150.1 50.5 reduce-scatter.2
  202.7 35.0 all-gather.8
  244.1 71.5 all-gather.10
  321.2 64.3 all-gather.12
  392.5 50.5 reduce-scatter.4
  445.1 35.0 all-gather.14
  486.4 71.4 all-gather.16
where the time goes:
time: 586 us; the launch traced here: 585 us
  waiting for transfers between devices  443 us (76%)
  blocking collectives  81.3 us (14%)
  matrix products  35.9 us (6%)
  between operations  14.3 us (2%)
  other arithmetic  8.14 us (1%)
    all_gather x2, waiting for transfers between devices, local(): lax.all_gather(first, 'col', axis=1, tiled=True)  143 us
    all_gather x2, waiting for transfers between devices, local(): gathered = lax.all_gather(current, 'col', axis=1, tiled=True)  128 us
    reduce_scatter x2, waiting for transfers between devices, local(): lax.psum_scatter(partial_gram, 'row', scatter_dimension=1, tiled=True)  101 us
    all_gather x2, waiting for transfers between devices, local(): gram_rows = lax.all_gather(shares, 'row', axis=1, tiled=True)  70.1 us
    psum x1, blocking collectives, local(): sumsq = lax.psum(jnp.sum(values * values), ('row', 'col'))  68.7 us
    dot_general x2, matrix products, local(): lax.dot_general(current, gathered, (((0,), (0,)), ((), ())), preferred_el...  13.6 us
    all_to_all x1, blocking collectives, local(): return lax.all_to_all(cube, 'col', split_axis=0, concat_axis=1, tiled=True)  12.7 us
    dot_general x2, matrix products, local(): lax.dot_general(gathered, gram_rows, (((1,), (1,)), ((), ())), preferred_...  12.3 us
  transfers between devices with their start and end apart: 8, of which 8 were waited for; matrix products, arithmetic and copies ran while one was open for 0% of the time, Pallas kernels for 0%

commit v1 on v0

v1 whole, which is shorter than its diff:
```python
import math

import jax
import jax.numpy as jnp
from jax import lax
from jax.sharding import Mesh
from jax.sharding import PartitionSpec as P

ITERS = 2
ROWS = 6144
COLS = 4096
BF = jnp.bfloat16
F32 = jnp.float32

AXES = ("xlo", "z", "y", "xhi", "core")


def pairs(move):
    out = []
    for xlo in range(2):
        for z in range(4):
            for y in range(4):
                for xhi in range(2):
                    for c in range(2):
                        x = 2 * xhi + xlo
                        x2, y2, z2, c2 = move(x, y, z, c)
                        x2, y2, z2, c2 = x2 % 4, y2 % 4, z2 % 4, c2 % 2
                        src = (((xlo * 4 + z) * 4 + y) * 2 + xhi) * 2 + c
                        dst = ((((x2 % 2) * 4 + z2) * 4 + y2) * 2 + x2 // 2) * 2 + c2
                        out.append((src, dst))
    return out


def permute(value, move):
    return lax.ppermute(value, AXES, pairs(move))


def swap_cores(value):
    return permute(value, lambda x, y, z, c: (x, y, z, 1 - c))


def from_y(value, j):
    return permute(value, lambda x, y, z, c: (x, y - j, z, c))


def to_major(value, d):
    return permute(value, lambda x, y, z, c: (x + d, y, z, c) if c == 0 else (x, y, z + d, c))


def to_minor(value, d):
    return permute(value, lambda x, y, z, c: (x, y, z + d, c) if c == 0 else (x + d, y, z, c))


def dot(a, b):
    return jnp.dot(a, b, preferred_element_type=F32)


def dot_t(a, b):
    return lax.dot_general(a, b, (((0,), (0,)), ((), ())), preferred_element_type=F32)


def gather_columns(block):
    arrived = {0: block}
    for j in (1, 3, 2):
        arrived[j] = from_y(block, j)
    return [jnp.concatenate([arrived[j], swap_cores(arrived[j])], axis=1) for j in range(4)]


def rows_at(value, index, size):
    return lax.dynamic_slice_in_dim(value, index * size, size, 0)


def place(blocks, first):
    size = blocks[0].shape[0]
    out = jnp.zeros((4 * size,) + blocks[0].shape[1:], blocks[0].dtype)
    for e, block in enumerate(blocks):
        out = lax.dynamic_update_slice_in_dim(out, block, ((first + e) % 4) * size, 0)
    return out


def local(unfolding):
    x_hi = lax.axis_index("xhi")
    x = 2 * x_hi + lax.axis_index("xlo")
    z = lax.axis_index("z")
    core = lax.axis_index("core")
    major = jnp.where(core == 0, x, z)
    minor = jnp.where(core == 0, z, x)

    half = unfolding.shape[0] // 2
    values = unfolding.astype(F32)
    sums = lax.psum(jnp.sum(values * values), AXES)
    factor = math.sqrt(COLS) / (3.0 * jnp.sqrt(sums))

    mine = lax.dynamic_slice_in_dim(unfolding, x_hi * half, half, 0)
    other = permute(
        lax.dynamic_slice_in_dim(unfolding, (1 - x_hi) * half, half, 0),
        lambda x, y, z, c: (x + 2, y, z, c),
    )
    current = jnp.concatenate(
        [jnp.where(x_hi == 0, mine, other), jnp.where(x_hi == 0, other, mine)], axis=1
    )
    scale = factor
    for turn_index in range(ITERS):
        blocks = gather_columns(current)
        whole = jnp.concatenate(blocks, axis=1)
        width = blocks[0].shape[1]
        slices = [
            lax.dynamic_slice_in_dim(whole, ((major + d) % 4) * width, width, 1) for d in range(4)
        ]
        total = dot_t(slices[0], current)
        for d in (1, 3, 2):
            total = total + to_major(dot_t(slices[d], current).astype(BF), d).astype(F32)
        piece = total.shape[0] // 4
        share = rows_at(total, minor, piece)
        for e in (1, 3, 2):
            share = share + to_minor(rows_at(total, (minor + e) % 4, piece).astype(BF), e).astype(F32)
        share = (share * (scale * scale)).astype(BF)
        quarter = place([share] + [to_minor(share, -e) for e in (1, 2, 3)], minor)
        gram = [quarter] + [to_major(quarter, -d) for d in (1, 2, 3)]
        first = dot(slices[0], gram[0])
        for d in (1, 3, 2):
            first = first + dot(slices[d], gram[d])
        first = (first * scale).astype(BF)
        ordered = place(gram, major)
        firsts = gather_columns(first)
        second = dot(firsts[0], rows_at(ordered, 0, width))
        for j in (1, 3, 2):
            second = second + dot(firsts[j], rows_at(ordered, j, width))
        updated = (
            (1.875 * scale) * current.astype(F32) - 1.25 * first.astype(F32) + 0.375 * second
        )
        current = updated.astype(BF)
        scale = jnp.float32(1.0)

    final = (updated * math.sqrt(ROWS)).astype(BF)
    pixels = final.shape[1] // 2
    parts = final.reshape(half, 2, 16, pixels // 16).transpose(2, 3, 1, 0)
    parts = lax.all_to_all(parts, ("y", "xhi", "core"), split_axis=0, concat_axis=0, tiled=True)
    parts = parts.reshape(4, 2, 2, pixels // 16, 2, half).transpose(3, 0, 4, 2, 1, 5)
    return parts.reshape(pixels // 16, 16, 2 * half)


def solution(mesh):
    wide = Mesh(mesh.devices.reshape(2, 4, 4, 2, 2), AXES)
    return jax.shard_map(
        local,
        mesh=wide,
        in_specs=(P(("xlo", "z"), ("y", "xhi", "core")),),
        out_specs=P(("y", "xhi", "core"), None, ("xlo", "z")),
        check_vma=False,
    )
```

time: 586 us -> 363 us (0.62)
  waiting for transfers between devices: 443 us -> 152 us
  starting transfers between devices: 0.48 us -> 88.8 us
  matrix products: 35.9 us -> 22 us
  between operations: 14.3 us -> 1.39 us
  local copies, waits for them, and re-layouts: 2.08 us -> 11.9 us
    all_gather x6 -> x0, waiting for transfers between devices: 341 us -> none  [the longest x2 143 us: local(): lax.all_gather(first, 'col', axis=1, tiled=True)]
    ppermute x0 -> x53, waiting for transfers between devices: none -> 152 us  [permute(): return lax.ppermute(value, AXES, pairs(move))]
    reduce_scatter x2 -> x0, waiting for transfers between devices: 101 us -> none  [local(): lax.psum_scatter(partial_gram, 'row', scatter_dimension=1, tiled=True)]
    ppermute x0 -> x53, starting transfers between devices: none -> 88.8 us  [permute(): return lax.ppermute(value, AXES, pairs(move))]
    dot_general x6 -> x24, matrix products: 35.9 us -> 22 us  [the longest x16 12.9 us: dot(): return jnp.dot(a, b, preferred_element_type=F32)]
    convert_element_type x4 -> x0, other arithmetic: 6.34 us -> none  [the longest x2 3.6 us: local(): lax.psum_scatter(partial_gram, 'row', scatter_dimension=1, tiled=True)]
  transfers between devices with their start and end apart: 8 -> 53, of which waited for: 8 -> 28; matrix products, arithmetic and copies ran while one was open for 0% -> 6% of each run, Pallas kernels for 0% -> 0%
where the time goes in v1:
time: 363 us; the launch traced here: 362 us
  waiting for transfers between devices  152 us (42%)
  starting transfers between devices  88.8 us (24%)
  blocking collectives  77.5 us (21%)
  matrix products  22 us (6%)
  local copies, waits for them, and re-layouts  11.9 us (3%)
  other arithmetic  8.23 us (2%)
    ppermute x53, waiting for transfers between devices, permute(): return lax.ppermute(value, AXES, pairs(move))  152 us
    ppermute x53, starting transfers between devices, permute(): return lax.ppermute(value, AXES, pairs(move))  88.8 us
    psum x1, blocking collectives, local(): sums = lax.psum(jnp.sum(values * values), AXES)  65 us
    dot_general x16, matrix products, dot(): return jnp.dot(a, b, preferred_element_type=F32)  12.9 us
    all_to_all x1, blocking collectives, local(): lax.all_to_all(parts, ('y', 'xhi', 'core'), split_axis=0, concat_axis=0,...  12.5 us
    dot_general x8, matrix products, dot_t(): lax.dot_general(a, b, (((0,), (0,)), ((), ())), preferred_element_type=F32)  9.17 us
  transfers between devices with their start and end apart: 53, of which 28 were waited for; matrix products, arithmetic and copies ran while one was open for 6% of the time, Pallas kernels for 0%

profile of v1, /device:TPU:1, one launch (start us, length us, event | category | flops | bytes accessed | tf_op | source)
XLA Modules:
  0.0 361.9 jit_solution(528863701093653274)
XLA Ops:
  0.9 3.7 %collective-permute-start = (bf16[384,256]{1,0:T(8,128)(2,1)S(1)}, bf16[384,256]{1,0:T(8,128)(2,1)S(1)}, u32[]{:S(2)}, u32[]{:S(2)}) collective-permute-start(bf16[384,256]{1,0:T(8,128)(2,1)S(1)} %constant_dynamic-slice_fusion), channel_id=1, source_target_pairs={{0,2},{1,3},{2,0},{3,1},{4,6},{5,7},{6,4},{7,5},{8,10},{9,11},{10,... | collective-permute-start | bytes 589832 | tf_op jit(solution)/shard_map/ppermute | solution.py:35
  4.6 4.2 %collective-permute-done = bf16[384,256]{1,0:T(8,128)(2,1)S(1)} collective-permute-done((bf16[384,256]{1,0:T(8,128)(2,1)S(1)}, bf16[384,256]{1,0:T(8,128)(2,1)S(1)}, u32[]{:S(2)}, u32[]{:S(2)}) %collective-permute-start) | collective-permute-done | bytes 196640 | tf_op jit(solution)/shard_map/ppermute | solution.py:35
  8.7 1.1 constant_dynamic-update-slice_fusion.8
  9.8 1.1 constant_dynamic-update-slice_fusion.7
  11.7 3.1 collective-permute-start.2
  15.8 2.4 collective-permute-start.1
  18.2 4.9 %collective-permute-done.2 = bf16[384,512]{1,0:T(8,128)(2,1)} collective-permute-done((bf16[384,512]{1,0:T(8,128)(2,1)}, bf16[384,512]{1,0:T(8,128)(2,1)}, u32[]{:S(2)}, u32[]{:S(2)}) %collective-permute-start.2) | collective-permute-done | bytes 393248 | tf_op jit(solution)/shard_map/ppermute | solution.py:35
  23.1 9.7 %collective-permute-start.3 = (bf16[384,512]{1,0:T(8,128)(2,1)}, bf16[384,512]{1,0:T(8,128)(2,1)}, u32[]{:S(2)}, u32[]{:S(2)}) collective-permute-start(bf16[384,512]{1,0:T(8,128)(2,1)} %collective-permute-done.2), channel_id=1, source_target_pairs={{0,1},{1,0},{2,3},{3,2},{4,5},{5,4},{6,7},{7,6},{8,9},{9,8},{10,11... | collective-permute-start | bytes 1179656 | tf_op jit(solution)/shard_map/ppermute | solution.py:35
  32.9 3.2 collective-permute-done.6
  37.6 1.0 constant_dynamic-update-slice_fusion.5
  42.0 1.9 convolution_convert_fusion.5
  43.9 1.6 collective-permute-start.8
  45.5 1.8 convolution_convert_fusion.4
  47.3 2.1 collective-permute-start.9
  49.5 1.7 convolution_convert_fusion.3
  51.2 1.3 collective-permute-start.10
  53.2 6.9 %collective-permute-done.8 = bf16[1024,512]{1,0:T(8,128)(2,1)} collective-permute-done((bf16[1024,512]{1,0:T(8,128)(2,1)}, bf16[1024,512]{1,0:T(8,128)(2,1)}, u32[]{:S(2)}, u32[]{:S(2)}) %collective-permute-start.8) | collective-permute-done | bytes 1048608 | tf_op jit(solution)/shard_map/ppermute | solution.py:35
  60.1 12.6 %collective-permute-done.9 = bf16[1024,512]{1,0:T(8,128)(2,1)} collective-permute-done((bf16[1024,512]{1,0:T(8,128)(2,1)}, bf16[1024,512]{1,0:T(8,128)(2,1)}, u32[]{:S(2)}, u32[]{:S(2)}) %collective-permute-start.9) | collective-permute-done | bytes 1048608 | tf_op jit(solution)/shard_map/ppermute | solution.py:35
  72.8 2.5 convert_add_fusion.1
  75.4 1.3 collective-permute-start.11
  76.7 1.5 collective-permute-start.12
  78.2 1.4 collective-permute-start.13
  80.4 65.0 %psum.7 = f32[]{:T(128)} all-reduce(f32[]{:T(128)} %multiply_reduce_fusion), channel_id=1, replica_groups=mesh['xlo'=2,'z'=4,'y'=4,'xhi'=2,'core'=2] {'xlo','z','y','xhi','core'}, use_global_device_ids=true, to_apply=%region_1.2 | all-reduce | flops 1 | bytes 8 | tf_op jit(solution)/shard_map/psum | solution.py:91
  146.9 1.3 constant_dynamic-update-slice_fusion.32
  148.2 1.9 collective-permute-start.14
  150.9 5.3 %collective-permute-done.14 = bf16[256,512]{1,0:T(8,128)(2,1)S(1)} collective-permute-done((bf16[256,512]{1,0:T(8,128)(2,1)S(1)}, bf16[256,512]{1,0:T(8,128)(2,1)S(1)}, u32[]{:S(2)}, u32[]{:S(2)}) %collective-permute-start.14) | collective-permute-done | bytes 262176 | tf_op jit(solution)/shard_map/ppermute | solution.py:35
  157.2 2.7 collective-permute-done.16
  162.4 11.6 %collective-permute-done.17 = bf16[1024,512]{1,0:T(8,128)(2,1)S(1)} collective-permute-done((bf16[1024,512]{1,0:T(8,128)(2,1)S(1)}, bf16[1024,512]{1,0:T(8,128)(2,1)S(1)}, u32[]{:S(2)}, u32[]{:S(2)}) %collective-permute-start.17) | collective-permute-done | bytes 1048608 | tf_op jit(solution)/shard_map/ppermute | solution.py:35
  174.0 1.7 fusion.70
  175.7 11.7 %collective-permute-done.18 = bf16[1024,512]{1,0:T(8,128)(2,1)S(1)} collective-permute-done((bf16[1024,512]{1,0:T(8,128)(2,1)S(1)}, bf16[1024,512]{1,0:T(8,128)(2,1)S(1)}, u32[]{:S(2)}, u32[]{:S(2)}) %collective-permute-start.18) | collective-permute-done | bytes 1048608 | tf_op jit(solution)/shard_map/ppermute | solution.py:35
  187.4 1.7 fusion.67
  189.1 1.8 fusion.64
  192.6 3.1 collective-permute-start.20
  195.7 2.6 collective-permute-start.21
  198.5 1.3 constant_dynamic-update-slice_fusion.26
  199.8 1.0 collective-permute-done.25
  200.9 7.1 %collective-permute-start.26 = (bf16[384,512]{1,0:T(8,128)(2,1)S(1)}, bf16[384,512]{1,0:T(8,128)(2,1)S(1)}, u32[]{:S(2)}, u32[]{:S(2)}) collective-permute-start(bf16[384,512]{1,0:T(8,128)(2,1)S(1)} %collective-permute-done.25), channel_id=1, source_target_pairs={{0,1},{1,0},{2,3},{3,2},{4,5},{5,4},{6,7},{7,6},{8,9},{9,8},{10,11... | collective-permute-start | bytes 1179656 | tf_op jit(solution)/shard_map/ppermute | solution.py:35
  208.1 1.9 collective-permute-done.21
  210.0 1.3 collective-permute-start.22
  211.3 1.7 collective-permute-done.23
  216.8 1.1 collective-permute-start.30
  218.8 8.2 %collective-permute-done.28 = bf16[384,512]{1,0:T(8,128)(2,1)S(1)} collective-permute-done((bf16[384,512]{1,0:T(8,128)(2,1)S(1)}, bf16[384,512]{1,0:T(8,128)(2,1)S(1)}, u32[]{:S(2)}, u32[]{:S(2)}) %collective-permute-start.28) | collective-permute-done | bytes 393248 | tf_op jit(solution)/shard_map/ppermute | solution.py:35
  227.0 1.2 collective-permute-start.29
  228.3 2.7 collective-permute-start.31
  231.0 6.8 %collective-permute-done.32 = bf16[384,512]{1,0:T(8,128)(2,1)S(1)} collective-permute-done((bf16[384,512]{1,0:T(8,128)(2,1)S(1)}, bf16[384,512]{1,0:T(8,128)(2,1)S(1)}, u32[]{:S(2)}, u32[]{:S(2)}) %collective-permute-start.32) | collective-permute-done | bytes 393248 | tf_op jit(solution)/shard_map/ppermute | solution.py:35
  242.0 2.7 collective-permute-start.35
  245.4 23.0 %collective-permute-done.34 = bf16[1024,512]{1,0:T(8,128)(2,1)S(1)} collective-permute-done((bf16[1024,512]{1,0:T(8,128)(2,1)S(1)}, bf16[1024,512]{1,0:T(8,128)(2,1)S(1)}, u32[]{:S(2)}, u32[]{:S(2)}) %collective-permute-start.34) | collective-permute-done | bytes 1048608 | tf_op jit(solution)/shard_map/ppermute | solution.py:35
  269.4 2.7 collective-permute-start.38
  272.0 4.0 %collective-permute-done.37 = bf16[256,512]{1,0:T(8,128)(2,1)S(1)} collective-permute-done((bf16[256,512]{1,0:T(8,128)(2,1)S(1)}, bf16[256,512]{1,0:T(8,128)(2,1)S(1)}, u32[]{:S(2)}, u32[]{:S(2)}) %collective-permute-start.37) | collective-permute-done | bytes 262176 | tf_op jit(solution)/shard_map/ppermute | solution.py:35
  276.1 2.1 collective-permute-done.38
  279.3 2.6 collective-permute-start.40
  282.5 5.5 %collective-permute-done.40 = bf16[256,512]{1,0:T(8,128)(2,1)S(1)} collective-permute-done((bf16[256,512]{1,0:T(8,128)(2,1)S(1)}, bf16[256,512]{1,0:T(8,128)(2,1)S(1)}, u32[]{:S(2)}, u32[]{:S(2)}) %collective-permute-start.40) | collective-permute-done | bytes 262176 | tf_op jit(solution)/shard_map/ppermute | solution.py:35
  288.7 2.7 collective-permute-done.42
  291.4 2.4 collective-permute-start.43
  293.9 1.3 collective-permute-start.45
  295.1 21.7 %collective-permute-done.43 = bf16[1024,512]{1,0:T(8,128)(2,1)S(1)} collective-permute-done((bf16[1024,512]{1,0:T(8,128)(2,1)S(1)}, bf16[1024,512]{1,0:T(8,128)(2,1)S(1)}, u32[]{:S(2)}, u32[]{:S(2)}) %collective-permute-start.43) | collective-permute-done | bytes 1048608 | tf_op jit(solution)/shard_map/ppermute | solution.py:35
  317.4 2.8 collective-permute-done.44
  322.0 1.2 collective-permute-start.51
  323.6 5.6 %collective-permute-start.46 = (bf16[384,512]{1,0:T(8,128)(2,1)S(1)}, bf16[384,512]{1,0:T(8,128)(2,1)S(1)}, u32[]{:S(2)}, u32[]{:S(2)}) collective-permute-start(bf16[384,512]{1,0:T(8,128)(2,1)S(1)} %fusion.13), channel_id=1, source_target_pairs={{0,1},{1,0},{2,3},{3,2},{4,5},{5,4},{6,7},{7,6},{8,9},{9,8},{10,11... | collective-permute-start | bytes 1179656 | tf_op jit(solution)/shard_map/ppermute | solution.py:35
  329.2 1.2 collective-permute-start.47
  330.9 8.1 %collective-permute-start.52 = (bf16[384,512]{1,0:T(8,128)(2,1)S(1)}, bf16[384,512]{1,0:T(8,128)(2,1)S(1)}, u32[]{:S(2)}, u32[]{:S(2)}) collective-permute-start(bf16[384,512]{1,0:T(8,128)(2,1)S(1)} %collective-permute-done.51), channel_id=1, source_target_pairs={{0,1},{1,0},{2,3},{3,2},{4,5},{5,4},{6,7},{7,6},{8,9},{9,8},{10,11... | collective-permute-start | bytes 1179656 | tf_op jit(solution)/shard_map/ppermute | solution.py:35
  339.0 2.8 collective-permute-done.47
  341.9 1.7 collective-permute-start.48
  348.0 12.5 %all_to_all.5 = bf16[16,16,2,384]{3,1,2,0:T(8,128)(2,1)S(1)} all-to-all(bf16[16,16,2,384]{3,1,2,0:T(8,128)(2,1)S(1)} %copy.6), channel_id=1, replica_groups=mesh['xlo'=2,'z'=4,'y'=4,'xhi'=2,'core'=2] {'y','xhi','core'}, dimensions={0} | all-to-all | bytes 786432 | tf_op jit(solution)/shard_map/all_to_all | solution.py:138
  (125 shorter events, 38.2 us)
Async XLA Ops:
  0.9 7.8 %collective-permute-start = (bf16[384,256]{1,0:T(8,128)(2,1)S(1)}, bf16[384,256]{1,0:T(8,128)(2,1)S(1)}, u32[]{:S(2)}, u32[]{:S(2)}) collective-permute-start(bf16[384,256]{1,0:T(8,128)(2,1)S(1)} %constant_dynamic-slice_fusion), channel_id=1, source_target_pairs={{0,2},{1,3},{2,0},{3,1},{4,6},{5,7},{6,4},{7,5},{8,10},{9,11},{10,... | collective-permute-start | bytes 589832 | tf_op jit(solution)/shard_map/ppermute | solution.py:35
  8.7 1.1 copy-start.3
  11.7 11.5 %collective-permute-start.2 = (bf16[384,512]{1,0:T(8,128)(2,1)}, bf16[384,512]{1,0:T(8,128)(2,1)}, u32[]{:S(2)}, u32[]{:S(2)}) collective-permute-start(bf16[384,512]{1,0:T(8,128)(2,1)} %pad_maximum_fusion), channel_id=1, source_target_pairs={{0,12},{1,13},{2,14},{3,15},{4,0},{5,1},{6,2},{7,3},{8,4},{9,5},{1... | collective-permute-start | bytes 1179656 | tf_op jit(solution)/shard_map/ppermute | solution.py:35
  14.8 18.1 %collective-permute-start.4 = (bf16[384,512]{1,0:T(8,128)(2,1)}, bf16[384,512]{1,0:T(8,128)(2,1)}, u32[]{:S(2)}, u32[]{:S(2)}) collective-permute-start(bf16[384,512]{1,0:T(8,128)(2,1)} %pad_maximum_fusion), channel_id=1, source_target_pairs={{0,8},{1,9},{2,10},{3,11},{4,12},{5,13},{6,14},{7,15},{8,0},{9,1},... | collective-permute-start | bytes 1179656 | tf_op jit(solution)/shard_map/ppermute | solution.py:35
  15.1 20.9 %collective-permute-start.6 = (bf16[384,512]{1,0:T(8,128)(2,1)}, bf16[384,512]{1,0:T(8,128)(2,1)}, u32[]{:S(2)}, u32[]{:S(2)}) collective-permute-start(bf16[384,512]{1,0:T(8,128)(2,1)} %pad_maximum_fusion), channel_id=1, source_target_pairs={{0,4},{1,5},{2,6},{3,7},{4,8},{5,9},{6,10},{7,11},{8,12},{9,13},{1... | collective-permute-start | bytes 1179656 | tf_op jit(solution)/shard_map/ppermute | solution.py:35
  15.8 20.7 %collective-permute-start.1 = (bf16[384,512]{1,0:T(8,128)(2,1)}, bf16[384,512]{1,0:T(8,128)(2,1)}, u32[]{:S(2)}, u32[]{:S(2)}) collective-permute-start(bf16[384,512]{1,0:T(8,128)(2,1)} %pad_maximum_fusion), channel_id=1, source_target_pairs={{0,1},{1,0},{2,3},{3,2},{4,5},{5,4},{6,7},{7,6},{8,9},{9,8},{10,11... | collective-permute-start | bytes 1179656 | tf_op jit(solution)/shard_map/ppermute | solution.py:35
  23.1 15.5 %collective-permute-start.3 = (bf16[384,512]{1,0:T(8,128)(2,1)}, bf16[384,512]{1,0:T(8,128)(2,1)}, u32[]{:S(2)}, u32[]{:S(2)}) collective-permute-start(bf16[384,512]{1,0:T(8,128)(2,1)} %collective-permute-done.2), channel_id=1, source_target_pairs={{0,1},{1,0},{2,3},{3,2},{4,5},{5,4},{6,7},{7,6},{8,9},{9,8},{10,11... | collective-permute-start | bytes 1179656 | tf_op jit(solution)/shard_map/ppermute | solution.py:35
  32.9 7.9 %collective-permute-start.5 = (bf16[384,512]{1,0:T(8,128)(2,1)}, bf16[384,512]{1,0:T(8,128)(2,1)S(1)}, u32[]{:S(2)}, u32[]{:S(2)}) collective-permute-start(bf16[384,512]{1,0:T(8,128)(2,1)} %collective-permute-done.4), channel_id=1, source_target_pairs={{0,1},{1,0},{2,3},{3,2},{4,5},{5,4},{6,7},{7,6},{8,9},{9,8},{10,11... | collective-permute-start | bytes 1179656 | tf_op jit(solution)/shard_map/ppermute | solution.py:35
  36.1 5.8 %collective-permute-start.7 = (bf16[384,512]{1,0:T(8,128)(2,1)}, bf16[384,512]{1,0:T(8,128)(2,1)S(1)}, u32[]{:S(2)}, u32[]{:S(2)}) collective-permute-start(bf16[384,512]{1,0:T(8,128)(2,1)} %collective-permute-done.6), channel_id=1, source_target_pairs={{0,1},{1,0},{2,3},{3,2},{4,5},{5,4},{6,7},{7,6},{8,9},{9,8},{10,11... | collective-permute-start | bytes 1179656 | tf_op jit(solution)/shard_map/ppermute | solution.py:35
  41.9 10.5 %copy-start = (bf16[384,4096]{1,0:T(8,128)(2,1)}, bf16[384,4096]{1,0:T(8,128)(2,1)S(1)}, u32[]{:S(2)}) copy-start(bf16[384,4096]{1,0:T(8,128)(2,1)S(1)} %constant_dynamic-update-slice_fusion) | copy-start | bytes 9437188
  43.9 16.3 %collective-permute-start.8 = (bf16[1024,512]{1,0:T(8,128)(2,1)}, bf16[1024,512]{1,0:T(8,128)(2,1)}, u32[]{:S(2)}, u32[]{:S(2)}) collective-permute-start(bf16[1024,512]{1,0:T(8,128)(2,1)} %convolution_convert_fusion.5), channel_id=1, source_target_pairs={{0,64},{1,17},{2,66},{3,19},{4,68},{5,21},{6,70},{7,23},{8,72},{9,... | collective-permute-start | bytes 3145736 | tf_op jit(solution)/shard_map/ppermute | solution.py:35
  47.3 25.4 %collective-permute-start.9 = (bf16[1024,512]{1,0:T(8,128)(2,1)}, bf16[1024,512]{1,0:T(8,128)(2,1)}, u32[]{:S(2)}, u32[]{:S(2)}) collective-permute-start(bf16[1024,512]{1,0:T(8,128)(2,1)} %convolution_convert_fusion.4), channel_id=1, source_target_pairs={{0,66},{1,49},{2,64},{3,51},{4,70},{5,53},{6,68},{7,55},{8,74},{9,... | collective-permute-start | bytes 3145736 | tf_op jit(solution)/shard_map/ppermute | solution.py:35
  51.2 21.6 %collective-permute-start.10 = (bf16[1024,512]{1,0:T(8,128)(2,1)}, bf16[1024,512]{1,0:T(8,128)(2,1)}, u32[]{:S(2)}, u32[]{:S(2)}) collective-permute-start(bf16[1024,512]{1,0:T(8,128)(2,1)} %convolution_convert_fusion.3), channel_id=1, source_target_pairs={{0,2},{1,33},{2,0},{3,35},{4,6},{5,37},{6,4},{7,39},{8,10},{9,41},... | collective-permute-start | bytes 3145736 | tf_op jit(solution)/shard_map/ppermute | solution.py:35
  53.2 26.4 %copy-start.2 = (bf16[768,256]{1,0:T(8,128)(2,1)S(1)}, bf16[768,256]{1,0:T(8,128)(2,1)}, u32[]{:S(2)}) copy-start(bf16[768,256]{1,0:T(8,128)(2,1)} %param.1) | copy-start | bytes 1179652
  75.4 70.7 %collective-permute-start.11 = (bf16[256,512]{1,0:T(8,128)(2,1)S(1)}, bf16[256,512]{1,0:T(8,128)(2,1)S(1)}, u32[]{:S(2)}, u32[]{:S(2)}) collective-permute-start(bf16[256,512]{1,0:T(8,128)(2,1)S(1)} %get-tuple-element.16), channel_id=1, source_target_pairs={{0,16},{1,65},{2,18},{3,67},{4,20},{5,69},{6,22},{7,71},{8,24},{9,... | collective-permute-start | bytes 786440 | tf_op jit(solution)/shard_map/ppermute | solution.py:35
  76.7 69.5 %collective-permute-start.12 = (bf16[256,512]{1,0:T(8,128)(2,1)S(1)}, bf16[256,512]{1,0:T(8,128)(2,1)}, u32[]{:S(2)}, u32[]{:S(2)}) collective-permute-start(bf16[256,512]{1,0:T(8,128)(2,1)S(1)} %get-tuple-element.18), channel_id=1, source_target_pairs={{0,48},{1,67},{2,50},{3,65},{4,52},{5,71},{6,54},{7,69},{8,56},{9,... | collective-permute-start | bytes 786440 | tf_op jit(solution)/shard_map/ppermute | solution.py:35
  78.2 68.7 %collective-permute-start.13 = (bf16[256,512]{1,0:T(8,128)(2,1)S(1)}, bf16[256,512]{1,0:T(8,128)(2,1)}, u32[]{:S(2)}, u32[]{:S(2)}) collective-permute-start(bf16[256,512]{1,0:T(8,128)(2,1)S(1)} %get-tuple-element.17), channel_id=1, source_target_pairs={{0,32},{1,3},{2,34},{3,1},{4,36},{5,7},{6,38},{7,5},{8,40},{9,11},... | collective-permute-start | bytes 786440 | tf_op jit(solution)/shard_map/ppermute | solution.py:35
  146.2 0.7 copy-start.4
  148.2 8.0 %collective-permute-start.14 = (bf16[256,512]{1,0:T(8,128)(2,1)S(1)}, bf16[256,512]{1,0:T(8,128)(2,1)S(1)}, u32[]{:S(2)}, u32[]{:S(2)}) collective-permute-start(bf16[256,512]{1,0:T(8,128)(2,1)S(1)} %get-tuple-element.8), channel_id=1, source_target_pairs={{0,48},{1,67},{2,50},{3,65},{4,52},{5,71},{6,54},{7,69},{8,56},{9,... | collective-permute-start | bytes 786440 | tf_op jit(solution)/shard_map/ppermute | solution.py:35
  150.1 7.1 %collective-permute-start.15 = (bf16[256,512]{1,0:T(8,128)(2,1)S(1)}, bf16[256,512]{1,0:T(8,128)(2,1)S(1)}, u32[]{:S(2)}, u32[]{:S(2)}) collective-permute-start(bf16[256,512]{1,0:T(8,128)(2,1)S(1)} %get-tuple-element.8), channel_id=1, source_target_pairs={{0,32},{1,3},{2,34},{3,1},{4,36},{5,7},{6,38},{7,5},{8,40},{9,11},... | collective-permute-start | bytes 786440 | tf_op jit(solution)/shard_map/ppermute | solution.py:35
  150.9 9.0 %collective-permute-start.16 = (bf16[256,512]{1,0:T(8,128)(2,1)S(1)}, bf16[256,512]{1,0:T(8,128)(2,1)S(1)}, u32[]{:S(2)}, u32[]{:S(2)}) collective-permute-start(bf16[256,512]{1,0:T(8,128)(2,1)S(1)} %get-tuple-element.8), channel_id=1, source_target_pairs={{0,16},{1,65},{2,18},{3,67},{4,20},{5,69},{6,22},{7,71},{8,24},{9,... | collective-permute-start | bytes 786440 | tf_op jit(solution)/shard_map/ppermute | solution.py:35
  160.0 14.0 %collective-permute-start.17 = (bf16[1024,512]{1,0:T(8,128)(2,1)S(1)}, bf16[1024,512]{1,0:T(8,128)(2,1)S(1)}, u32[]{:S(2)}, u32[]{:S(2)}) collective-permute-start(bf16[1024,512]{1,0:T(8,128)(2,1)S(1)} %constant_dynamic-update-slice_fusion.29), channel_id=1, source_target_pairs={{0,66},{1,49},{2,64},{3,51},{4,70},{5,53},{6,68},{7,55},{8,74},{9,... | collective-permute-start | bytes 3145736 | tf_op jit(solution)/shard_map/ppermute | solution.py:35
  160.9 26.5 %collective-permute-start.18 = (bf16[1024,512]{1,0:T(8,128)(2,1)S(1)}, bf16[1024,512]{1,0:T(8,128)(2,1)S(1)}, u32[]{:S(2)}, u32[]{:S(2)}) collective-permute-start(bf16[1024,512]{1,0:T(8,128)(2,1)S(1)} %constant_dynamic-update-slice_fusion.29), channel_id=1, source_target_pairs={{0,64},{1,17},{2,66},{3,19},{4,68},{5,21},{6,70},{7,23},{8,72},{9,... | collective-permute-start | bytes 3145736 | tf_op jit(solution)/shard_map/ppermute | solution.py:35
  161.5 27.6 %collective-permute-start.19 = (bf16[1024,512]{1,0:T(8,128)(2,1)S(1)}, bf16[1024,512]{1,0:T(8,128)(2,1)}, u32[]{:S(2)}, u32[]{:S(2)}) collective-permute-start(bf16[1024,512]{1,0:T(8,128)(2,1)S(1)} %constant_dynamic-update-slice_fusion.29), channel_id=1, source_target_pairs={{0,2},{1,33},{2,0},{3,35},{4,6},{5,37},{6,4},{7,39},{8,10},{9,41},... | collective-permute-start | bytes 3145736 | tf_op jit(solution)/shard_map/ppermute | solution.py:35
  162.4 26.7 %copy-start.1 = (bf16[384,4096]{1,0:T(8,128)(2,1)S(1)}, bf16[384,4096]{1,0:T(8,128)(2,1)}, u32[]{:S(2)}) copy-start(bf16[384,4096]{1,0:T(8,128)(2,1)} %copy-done) | copy-start | bytes 9437188
  191.5 9.4 %collective-permute-start.25 = (bf16[384,512]{1,0:T(8,128)(2,1)S(1)}, bf16[384,512]{1,0:T(8,128)(2,1)S(1)}, u32[]{:S(2)}, u32[]{:S(2)}) collective-permute-start(bf16[384,512]{1,0:T(8,128)(2,1)S(1)} %fusion.15), channel_id=1, source_target_pairs={{0,8},{1,9},{2,10},{3,11},{4,12},{5,13},{6,14},{7,15},{8,0},{9,1},... | collective-permute-start | bytes 1179656 | tf_op jit(solution)/shard_map/ppermute | solution.py:35
  192.6 21.2 %collective-permute-start.20 = (bf16[384,512]{1,0:T(8,128)(2,1)S(1)}, bf16[384,512]{1,0:T(8,128)(2,1)S(1)}, u32[]{:S(2)}, u32[]{:S(2)}) collective-permute-start(bf16[384,512]{1,0:T(8,128)(2,1)S(1)} %fusion.15), channel_id=1, source_target_pairs={{0,1},{1,0},{2,3},{3,2},{4,5},{5,4},{6,7},{7,6},{8,9},{9,8},{10,11... | collective-permute-start | bytes 1179656 | tf_op jit(solution)/shard_map/ppermute | solution.py:35
  195.7 14.3 %collective-permute-start.21 = (bf16[384,512]{1,0:T(8,128)(2,1)S(1)}, bf16[384,512]{1,0:T(8,128)(2,1)S(1)}, u32[]{:S(2)}, u32[]{:S(2)}) collective-permute-start(bf16[384,512]{1,0:T(8,128)(2,1)S(1)} %fusion.15), channel_id=1, source_target_pairs={{0,12},{1,13},{2,14},{3,15},{4,0},{5,1},{6,2},{7,3},{8,4},{9,5},{1... | collective-permute-start | bytes 1179656 | tf_op jit(solution)/shard_map/ppermute | solution.py:35
  198.4 14.6 %collective-permute-start.23 = (bf16[384,512]{1,0:T(8,128)(2,1)S(1)}, bf16[384,512]{1,0:T(8,128)(2,1)S(1)}, u32[]{:S(2)}, u32[]{:S(2)}) collective-permute-start(bf16[384,512]{1,0:T(8,128)(2,1)S(1)} %fusion.15), channel_id=1, source_target_pairs={{0,4},{1,5},{2,6},{3,7},{4,8},{5,9},{6,10},{7,11},{8,12},{9,13},{1... | collective-permute-start | bytes 1179656 | tf_op jit(solution)/shard_map/ppermute | solution.py:35
  200.9 13.5 %collective-permute-start.26 = (bf16[384,512]{1,0:T(8,128)(2,1)S(1)}, bf16[384,512]{1,0:T(8,128)(2,1)S(1)}, u32[]{:S(2)}, u32[]{:S(2)}) collective-permute-start(bf16[384,512]{1,0:T(8,128)(2,1)S(1)} %collective-permute-done.25), channel_id=1, source_target_pairs={{0,1},{1,0},{2,3},{3,2},{4,5},{5,4},{6,7},{7,6},{8,9},{9,8},{10,11... | collective-permute-start | bytes 1179656 | tf_op jit(solution)/shard_map/ppermute | solution.py:35
  210.0 4.9 %collective-permute-start.22 = (bf16[384,512]{1,0:T(8,128)(2,1)S(1)}, bf16[384,512]{1,0:T(8,128)(2,1)S(1)}, u32[]{:S(2)}, u32[]{:S(2)}) collective-permute-start(bf16[384,512]{1,0:T(8,128)(2,1)S(1)} %collective-permute-done.21), channel_id=1, source_target_pairs={{0,1},{1,0},{2,3},{3,2},{4,5},{5,4},{6,7},{7,6},{8,9},{9,8},{10,11... | collective-permute-start | bytes 1179656 | tf_op jit(solution)/shard_map/ppermute | solution.py:35
  213.0 2.5 collective-permute-start.24
  216.2 10.8 %collective-permute-start.28 = (bf16[384,512]{1,0:T(8,128)(2,1)S(1)}, bf16[384,512]{1,0:T(8,128)(2,1)S(1)}, u32[]{:S(2)}, u32[]{:S(2)}) collective-permute-start(bf16[384,512]{1,0:T(8,128)(2,1)S(1)} %get-tuple-element.20), channel_id=1, source_target_pairs={{0,12},{1,13},{2,14},{3,15},{4,0},{5,1},{6,2},{7,3},{8,4},{9,5},{1... | collective-permute-start | bytes 1179656 | tf_op jit(solution)/shard_map/ppermute | solution.py:35
  216.8 11.5 %collective-permute-start.30 = (bf16[384,512]{1,0:T(8,128)(2,1)S(1)}, bf16[384,512]{1,0:T(8,128)(2,1)S(1)}, u32[]{:S(2)}, u32[]{:S(2)}) collective-permute-start(bf16[384,512]{1,0:T(8,128)(2,1)S(1)} %get-tuple-element.20), channel_id=1, source_target_pairs={{0,8},{1,9},{2,10},{3,11},{4,12},{5,13},{6,14},{7,15},{8,0},{9,1},... | collective-permute-start | bytes 1179656 | tf_op jit(solution)/shard_map/ppermute | solution.py:35
  217.9 19.8 %collective-permute-start.32 = (bf16[384,512]{1,0:T(8,128)(2,1)S(1)}, bf16[384,512]{1,0:T(8,128)(2,1)S(1)}, u32[]{:S(2)}, u32[]{:S(2)}) collective-permute-start(bf16[384,512]{1,0:T(8,128)(2,1)S(1)} %get-tuple-element.20), channel_id=1, source_target_pairs={{0,4},{1,5},{2,6},{3,7},{4,8},{5,9},{6,10},{7,11},{8,12},{9,13},{1... | collective-permute-start | bytes 1179656 | tf_op jit(solution)/shard_map/ppermute | solution.py:35
  217.9 20.3 %collective-permute-start.27 = (bf16[384,512]{1,0:T(8,128)(2,1)S(1)}, bf16[384,512]{1,0:T(8,128)(2,1)S(1)}, u32[]{:S(2)}, u32[]{:S(2)}) collective-permute-start(bf16[384,512]{1,0:T(8,128)(2,1)S(1)} %get-tuple-element.20), channel_id=1, source_target_pairs={{0,1},{1,0},{2,3},{3,2},{4,5},{5,4},{6,7},{7,6},{8,9},{9,8},{10,11... | collective-permute-start | bytes 1179656 | tf_op jit(solution)/shard_map/ppermute | solution.py:35
  227.0 11.3 %collective-permute-start.29 = (bf16[384,512]{1,0:T(8,128)(2,1)S(1)}, bf16[384,512]{1,0:T(8,128)(2,1)S(1)}, u32[]{:S(2)}, u32[]{:S(2)}) collective-permute-start(bf16[384,512]{1,0:T(8,128)(2,1)S(1)} %collective-permute-done.28), channel_id=1, source_target_pairs={{0,1},{1,0},{2,3},{3,2},{4,5},{5,4},{6,7},{7,6},{8,9},{9,8},{10,11... | collective-permute-start | bytes 1179656 | tf_op jit(solution)/shard_map/ppermute | solution.py:35
  228.3 10.1 %collective-permute-start.31 = (bf16[384,512]{1,0:T(8,128)(2,1)S(1)}, bf16[384,512]{1,0:T(8,128)(2,1)S(1)}, u32[]{:S(2)}, u32[]{:S(2)}) collective-permute-start(bf16[384,512]{1,0:T(8,128)(2,1)S(1)} %collective-permute-done.30), channel_id=1, source_target_pairs={{0,1},{1,0},{2,3},{3,2},{4,5},{5,4},{6,7},{7,6},{8,9},{9,8},{10,11... | collective-permute-start | bytes 1179656 | tf_op jit(solution)/shard_map/ppermute | solution.py:35
  237.7 1.8 collective-permute-start.33
  241.9 26.5 %collective-permute-start.34 = (bf16[1024,512]{1,0:T(8,128)(2,1)S(1)}, bf16[1024,512]{1,0:T(8,128)(2,1)S(1)}, u32[]{:S(2)}, u32[]{:S(2)}) collective-permute-start(bf16[1024,512]{1,0:T(8,128)(2,1)S(1)} %convolution_convert_fusion.2), channel_id=1, source_target_pairs={{0,64},{1,17},{2,66},{3,19},{4,68},{5,21},{6,70},{7,23},{8,72},{9,... | collective-permute-start | bytes 3145736 | tf_op jit(solution)/shard_map/ppermute | solution.py:35
  242.0 26.4 %collective-permute-start.35 = (bf16[1024,512]{1,0:T(8,128)(2,1)S(1)}, bf16[1024,512]{1,0:T(8,128)(2,1)S(1)}, u32[]{:S(2)}, u32[]{:S(2)}) collective-permute-start(bf16[1024,512]{1,0:T(8,128)(2,1)S(1)} %convolution_convert_fusion.1), channel_id=1, source_target_pairs={{0,66},{1,49},{2,64},{3,51},{4,70},{5,53},{6,68},{7,55},{8,74},{9,... | collective-permute-start | bytes 3145736 | tf_op jit(solution)/shard_map/ppermute | solution.py:35
  244.6 23.7 %collective-permute-start.36 = (bf16[1024,512]{1,0:T(8,128)(2,1)S(1)}, bf16[1024,512]{1,0:T(8,128)(2,1)S(1)}, u32[]{:S(2)}, u32[]{:S(2)}) collective-permute-start(bf16[1024,512]{1,0:T(8,128)(2,1)S(1)} %convolution_convert_fusion), channel_id=1, source_target_pairs={{0,2},{1,33},{2,0},{3,35},{4,6},{5,37},{6,4},{7,39},{8,10},{9,41},... | collective-permute-start | bytes 3145736 | tf_op jit(solution)/shard_map/ppermute | solution.py:35
  269.1 7.0 %collective-permute-start.37 = (bf16[256,512]{1,0:T(8,128)(2,1)S(1)}, bf16[256,512]{1,0:T(8,128)(2,1)S(1)}, u32[]{:S(2)}, u32[]{:S(2)}) collective-permute-start(bf16[256,512]{1,0:T(8,128)(2,1)S(1)} %get-tuple-element.13), channel_id=1, source_target_pairs={{0,16},{1,65},{2,18},{3,67},{4,20},{5,69},{6,22},{7,71},{8,24},{9,... | collective-permute-start | bytes 786440 | tf_op jit(solution)/shard_map/ppermute | solution.py:35
  269.4 8.8 %collective-permute-start.38 = (bf16[256,512]{1,0:T(8,128)(2,1)S(1)}, bf16[256,512]{1,0:T(8,128)(2,1)S(1)}, u32[]{:S(2)}, u32[]{:S(2)}) collective-permute-start(bf16[256,512]{1,0:T(8,128)(2,1)S(1)} %get-tuple-element.15), channel_id=1, source_target_pairs={{0,48},{1,67},{2,50},{3,65},{4,52},{5,71},{6,54},{7,69},{8,56},{9,... | collective-permute-start | bytes 786440 | tf_op jit(solution)/shard_map/ppermute | solution.py:35
  272.0 7.0 %collective-permute-start.39 = (bf16[256,512]{1,0:T(8,128)(2,1)S(1)}, bf16[256,512]{1,0:T(8,128)(2,1)S(1)}, u32[]{:S(2)}, u32[]{:S(2)}) collective-permute-start(bf16[256,512]{1,0:T(8,128)(2,1)S(1)} %get-tuple-element.14), channel_id=1, source_target_pairs={{0,32},{1,3},{2,34},{3,1},{4,36},{5,7},{6,38},{7,5},{8,40},{9,11},... | collective-permute-start | bytes 786440 | tf_op jit(solution)/shard_map/ppermute | solution.py:35
  279.3 8.7 %collective-permute-start.40 = (bf16[256,512]{1,0:T(8,128)(2,1)S(1)}, bf16[256,512]{1,0:T(8,128)(2,1)S(1)}, u32[]{:S(2)}, u32[]{:S(2)}) collective-permute-start(bf16[256,512]{1,0:T(8,128)(2,1)S(1)} %get-tuple-element.6), channel_id=1, source_target_pairs={{0,48},{1,67},{2,50},{3,65},{4,52},{5,71},{6,54},{7,69},{8,56},{9,... | collective-permute-start | bytes 786440 | tf_op jit(solution)/shard_map/ppermute | solution.py:35
  281.9 6.8 %collective-permute-start.41 = (bf16[256,512]{1,0:T(8,128)(2,1)S(1)}, bf16[256,512]{1,0:T(8,128)(2,1)S(1)}, u32[]{:S(2)}, u32[]{:S(2)}) collective-permute-start(bf16[256,512]{1,0:T(8,128)(2,1)S(1)} %get-tuple-element.6), channel_id=1, source_target_pairs={{0,32},{1,3},{2,34},{3,1},{4,36},{5,7},{6,38},{7,5},{8,40},{9,11},... | collective-permute-start | bytes 786440 | tf_op jit(solution)/shard_map/ppermute | solution.py:35
  281.9 9.5 %collective-permute-start.42 = (bf16[256,512]{1,0:T(8,128)(2,1)S(1)}, bf16[256,512]{1,0:T(8,128)(2,1)S(1)}, u32[]{:S(2)}, u32[]{:S(2)}) collective-permute-start(bf16[256,512]{1,0:T(8,128)(2,1)S(1)} %get-tuple-element.6), channel_id=1, source_target_pairs={{0,16},{1,65},{2,18},{3,67},{4,20},{5,69},{6,22},{7,71},{8,24},{9,... | collective-permute-start | bytes 786440 | tf_op jit(solution)/shard_map/ppermute | solution.py:35
  291.4 25.4 %collective-permute-start.43 = (bf16[1024,512]{1,0:T(8,128)(2,1)S(1)}, bf16[1024,512]{1,0:T(8,128)(2,1)S(1)}, u32[]{:S(2)}, u32[]{:S(2)}) collective-permute-start(bf16[1024,512]{1,0:T(8,128)(2,1)S(1)} %constant_dynamic-update-slice_fusion.21), channel_id=1, source_target_pairs={{0,66},{1,49},{2,64},{3,51},{4,70},{5,53},{6,68},{7,55},{8,74},{9,... | collective-permute-start | bytes 3145736 | tf_op jit(solution)/shard_map/ppermute | solution.py:35
  293.9 26.4 %collective-permute-start.44 = (bf16[1024,512]{1,0:T(8,128)(2,1)S(1)}, bf16[1024,512]{1,0:T(8,128)(2,1)S(1)}, u32[]{:S(2)}, u32[]{:S(2)}) collective-permute-start(bf16[1024,512]{1,0:T(8,128)(2,1)S(1)} %constant_dynamic-update-slice_fusion.21), channel_id=1, source_target_pairs={{0,64},{1,17},{2,66},{3,19},{4,68},{5,21},{6,70},{7,23},{8,72},{9,... | collective-permute-start | bytes 3145736 | tf_op jit(solution)/shard_map/ppermute | solution.py:35
  293.9 27.0 %collective-permute-start.45 = (bf16[1024,512]{1,0:T(8,128)(2,1)S(1)}, bf16[1024,512]{1,0:T(8,128)(2,1)S(1)}, u32[]{:S(2)}, u32[]{:S(2)}) collective-permute-start(bf16[1024,512]{1,0:T(8,128)(2,1)S(1)} %constant_dynamic-update-slice_fusion.21), channel_id=1, source_target_pairs={{0,2},{1,33},{2,0},{3,35},{4,6},{5,37},{6,4},{7,39},{8,10},{9,41},... | collective-permute-start | bytes 3145736 | tf_op jit(solution)/shard_map/ppermute | solution.py:35
  322.0 8.9 %collective-permute-start.51 = (bf16[384,512]{1,0:T(8,128)(2,1)S(1)}, bf16[384,512]{1,0:T(8,128)(2,1)S(1)}, u32[]{:S(2)}, u32[]{:S(2)}) collective-permute-start(bf16[384,512]{1,0:T(8,128)(2,1)S(1)} %fusion.13), channel_id=1, source_target_pairs={{0,8},{1,9},{2,10},{3,11},{4,12},{5,13},{6,14},{7,15},{8,0},{9,1},... | collective-permute-start | bytes 1179656 | tf_op jit(solution)/shard_map/ppermute | solution.py:35
  323.6 21.7 %collective-permute-start.46 = (bf16[384,512]{1,0:T(8,128)(2,1)S(1)}, bf16[384,512]{1,0:T(8,128)(2,1)S(1)}, u32[]{:S(2)}, u32[]{:S(2)}) collective-permute-start(bf16[384,512]{1,0:T(8,128)(2,1)S(1)} %fusion.13), channel_id=1, source_target_pairs={{0,1},{1,0},{2,3},{3,2},{4,5},{5,4},{6,7},{7,6},{8,9},{9,8},{10,11... | collective-permute-start | bytes 1179656 | tf_op jit(solution)/shard_map/ppermute | solution.py:35
  329.2 12.7 %collective-permute-start.47 = (bf16[384,512]{1,0:T(8,128)(2,1)S(1)}, bf16[384,512]{1,0:T(8,128)(2,1)S(1)}, u32[]{:S(2)}, u32[]{:S(2)}) collective-permute-start(bf16[384,512]{1,0:T(8,128)(2,1)S(1)} %fusion.13), channel_id=1, source_target_pairs={{0,12},{1,13},{2,14},{3,15},{4,0},{5,1},{6,2},{7,3},{8,4},{9,5},{1... | collective-permute-start | bytes 1179656 | tf_op jit(solution)/shard_map/ppermute | solution.py:35
  330.4 14.1 %collective-permute-start.49 = (bf16[384,512]{1,0:T(8,128)(2,1)S(1)}, bf16[384,512]{1,0:T(8,128)(2,1)S(1)}, u32[]{:S(2)}, u32[]{:S(2)}) collective-permute-start(bf16[384,512]{1,0:T(8,128)(2,1)S(1)} %fusion.13), channel_id=1, source_target_pairs={{0,4},{1,5},{2,6},{3,7},{4,8},{5,9},{6,10},{7,11},{8,12},{9,13},{1... | collective-permute-start | bytes 1179656 | tf_op jit(solution)/shard_map/ppermute | solution.py:35
  330.9 15.0 %collective-permute-start.52 = (bf16[384,512]{1,0:T(8,128)(2,1)S(1)}, bf16[384,512]{1,0:T(8,128)(2,1)S(1)}, u32[]{:S(2)}, u32[]{:S(2)}) collective-permute-start(bf16[384,512]{1,0:T(8,128)(2,1)S(1)} %collective-permute-done.51), channel_id=1, source_target_pairs={{0,1},{1,0},{2,3},{3,2},{4,5},{5,4},{6,7},{7,6},{8,9},{9,8},{10,11... | collective-permute-start | bytes 1179656 | tf_op jit(solution)/shard_map/ppermute | solution.py:35
  341.9 4.5 %collective-permute-start.48 = (bf16[384,512]{1,0:T(8,128)(2,1)S(1)}, bf16[384,512]{1,0:T(8,128)(2,1)S(1)}, u32[]{:S(2)}, u32[]{:S(2)}) collective-permute-start(bf16[384,512]{1,0:T(8,128)(2,1)S(1)} %collective-permute-done.47), channel_id=1, source_target_pairs={{0,1},{1,0},{2,3},{3,2},{4,5},{5,4},{6,7},{7,6},{8,9},{9,8},{10,11... | collective-permute-start | bytes 1179656 | tf_op jit(solution)/shard_map/ppermute | solution.py:35
  344.5 2.5 collective-permute-start.50

commit v2 on v1

--- a/solution.py
+++ b/solution.py
@@ -51,6 +51,20 @@
     return permute(value, lambda x, y, z, c: (x, y, z + d, c) if c == 0 else (x + d, y, z, c))
 
 
+def sum_over_all(value):
+    for move in (
+        lambda x, y, z, c: (x, y, z, 1 - c),
+        lambda x, y, z, c: (x, y ^ 1, z, c),
+        lambda x, y, z, c: (x, y ^ 2, z, c),
+        lambda x, y, z, c: (x ^ 1, y, z, c),
+        lambda x, y, z, c: (x ^ 2, y, z, c),
+        lambda x, y, z, c: (x, y, z ^ 1, c),
+        lambda x, y, z, c: (x, y, z ^ 2, c),
+    ):
+        value = value + permute(value, move)
+    return value
+
+
 def dot(a, b):
     return jnp.dot(a, b, preferred_element_type=F32)
 
@@ -88,7 +102,7 @@
 
     half = unfolding.shape[0] // 2
     values = unfolding.astype(F32)
-    sums = lax.psum(jnp.sum(values * values), AXES)
+    sums = jnp.sum(sum_over_all(jnp.sum((values * values).reshape(-1, 8, 2, 128), axis=(0, 2))))
     factor = math.sqrt(COLS) / (3.0 * jnp.sqrt(sums))
 
     mine = lax.dynamic_slice_in_dim(unfolding, x_hi * half, half, 0)

time: 363 us -> 329 us (0.906)
  blocking collectives: 77.5 us -> 12.6 us
  starting transfers between devices: 88.8 us -> 108 us
  waiting for transfers between devices: 152 us -> 164 us
    psum x1 -> x0, blocking collectives: 65 us -> none  [local(): sums = lax.psum(jnp.sum(values * values), AXES)]
    ppermute x53 -> x60, starting transfers between devices: 88.8 us -> 108 us  [permute(): return lax.ppermute(value, AXES, pairs(move))]
    ppermute x53 -> x60, waiting for transfers between devices: 152 us -> 164 us  [permute(): return lax.ppermute(value, AXES, pairs(move))]
  transfers between devices with their start and end apart: 53 -> 60, of which waited for: 28 -> 35; matrix products, arithmetic and copies ran while one was open for 6% -> 7% of each run, Pallas kernels for 0% -> 0%
where the time goes in v2:
time: 329 us; the launch traced here: 328 us
  waiting for transfers between devices  164 us (50%)
  starting transfers between devices  108 us (33%)
  matrix products  22 us (7%)
  blocking collectives  12.6 us (4%)
  local copies, waits for them, and re-layouts  11.9 us (4%)
  other arithmetic  8.25 us (3%)
    ppermute x60, waiting for transfers between devices, permute(): return lax.ppermute(value, AXES, pairs(move))  164 us
    ppermute x60, starting transfers between devices, permute(): return lax.ppermute(value, AXES, pairs(move))  108 us
    dot_general x16, matrix products, dot(): return jnp.dot(a, b, preferred_element_type=F32)  12.9 us
    all_to_all x1, blocking collectives, local(): lax.all_to_all(parts, ('y', 'xhi', 'core'), split_axis=0, concat_axis=0,...  12.6 us
    dot_general x8, matrix products, dot_t(): lax.dot_general(a, b, (((0,), (0,)), ((), ())), preferred_element_type=F32)  9.16 us
  transfers between devices with their start and end apart: 60, of which 35 were waited for; matrix products, arithmetic and copies ran while one was open for 7% of the time, Pallas kernels for 0%

profile of v2, /device:TPU:1, one launch (start us, length us, event | category | flops | bytes accessed | tf_op | source)
XLA Modules:
  0.0 328.1 jit_solution(14487532927744169563)
XLA Ops:
  0.9 3.7 %collective-permute-start.7 = (bf16[384,256]{1,0:T(8,128)(2,1)S(1)}, bf16[384,256]{1,0:T(8,128)(2,1)S(1)}, u32[]{:S(2)}, u32[]{:S(2)}) collective-permute-start(bf16[384,256]{1,0:T(8,128)(2,1)S(1)} %constant_dynamic-slice_fusion), channel_id=1, source_target_pairs={{0,2},{1,3},{2,0},{3,1},{4,6},{5,7},{6,4},{7,5},{8,10},{9,11},{10,... | collective-permute-start | bytes 589832 | tf_op jit(solution)/shard_map/ppermute | solution.py:35
  4.6 4.2 %collective-permute-done.7 = bf16[384,256]{1,0:T(8,128)(2,1)S(1)} collective-permute-done((bf16[384,256]{1,0:T(8,128)(2,1)S(1)}, bf16[384,256]{1,0:T(8,128)(2,1)S(1)}, u32[]{:S(2)}, u32[]{:S(2)}) %collective-permute-start.7) | collective-permute-done | bytes 196640 | tf_op jit(solution)/shard_map/ppermute | solution.py:35
  11.7 3.1 collective-permute-start.9
  15.8 2.4 collective-permute-start.8
  18.2 4.9 %collective-permute-done.9 = bf16[384,512]{1,0:T(8,128)(2,1)} collective-permute-done((bf16[384,512]{1,0:T(8,128)(2,1)}, bf16[384,512]{1,0:T(8,128)(2,1)}, u32[]{:S(2)}, u32[]{:S(2)}) %collective-permute-start.9) | collective-permute-done | bytes 393248 | tf_op jit(solution)/shard_map/ppermute | solution.py:35
  23.1 9.7 %collective-permute-start.10 = (bf16[384,512]{1,0:T(8,128)(2,1)}, bf16[384,512]{1,0:T(8,128)(2,1)}, u32[]{:S(2)}, u32[]{:S(2)}) collective-permute-start(bf16[384,512]{1,0:T(8,128)(2,1)} %collective-permute-done.9), channel_id=1, source_target_pairs={{0,1},{1,0},{2,3},{3,2},{4,5},{5,4},{6,7},{7,6},{8,9},{9,8},{10,11... | collective-permute-start | bytes 1179656 | tf_op jit(solution)/shard_map/ppermute | solution.py:35
  32.9 3.2 collective-permute-done.13
  42.0 1.9 convolution_convert_fusion.5
  43.9 1.6 collective-permute-start.15
  45.5 1.8 convolution_convert_fusion.4
  47.3 2.1 collective-permute-start.16
  49.5 1.7 convolution_convert_fusion.3
  51.2 1.3 collective-permute-start.17
  53.2 6.9 %collective-permute-done.15 = bf16[1024,512]{1,0:T(8,128)(2,1)} collective-permute-done((bf16[1024,512]{1,0:T(8,128)(2,1)}, bf16[1024,512]{1,0:T(8,128)(2,1)}, u32[]{:S(2)}, u32[]{:S(2)}) %collective-permute-start.15) | collective-permute-done | bytes 1048608 | tf_op jit(solution)/shard_map/ppermute | solution.py:35
  60.2 12.6 %collective-permute-done.16 = bf16[1024,512]{1,0:T(8,128)(2,1)} collective-permute-done((bf16[1024,512]{1,0:T(8,128)(2,1)}, bf16[1024,512]{1,0:T(8,128)(2,1)}, u32[]{:S(2)}, u32[]{:S(2)}) %collective-permute-start.16) | collective-permute-done | bytes 1048608 | tf_op jit(solution)/shard_map/ppermute | solution.py:35
  72.8 2.5 convert_add_fusion.1
  75.4 1.3 collective-permute-start.18
  76.7 1.5 collective-permute-start.19
  78.2 1.4 collective-permute-start.20
  79.8 1.9 collective-permute-start
  82.6 2.9 collective-permute-done.1
  85.4 4.0 %collective-permute-done.2 = f32[8,128]{1,0:T(8,128)S(1)} collective-permute-done((f32[8,128]{1,0:T(8,128)S(1)}, f32[8,128]{1,0:T(8,128)S(1)}, u32[]{:S(2)}, u32[]{:S(2)}) %collective-permute-start.2) | collective-permute-done | bytes 4128 | tf_op jit(solution)/shard_map/ppermute | solution.py:35
  89.4 2.5 collective-permute-start.3
  92.9 2.1 collective-permute-start.4
  95.0 1.9 collective-permute-done.4
  97.2 2.1 collective-permute-done.5
  99.3 1.5 collective-permute-start.6
  100.8 2.5 collective-permute-done.6
  105.4 1.3 constant_dynamic-update-slice_fusion.32
  106.7 2.5 collective-permute-start.21
  110.0 5.3 %collective-permute-done.21 = bf16[256,512]{1,0:T(8,128)(2,1)S(1)} collective-permute-done((bf16[256,512]{1,0:T(8,128)(2,1)S(1)}, bf16[256,512]{1,0:T(8,128)(2,1)S(1)}, u32[]{:S(2)}, u32[]{:S(2)}) %collective-permute-start.21) | collective-permute-done | bytes 262176 | tf_op jit(solution)/shard_map/ppermute | solution.py:35
  116.0 3.0 collective-permute-done.23
  121.7 11.6 %collective-permute-done.24 = bf16[1024,512]{1,0:T(8,128)(2,1)S(1)} collective-permute-done((bf16[1024,512]{1,0:T(8,128)(2,1)S(1)}, bf16[1024,512]{1,0:T(8,128)(2,1)S(1)}, u32[]{:S(2)}, u32[]{:S(2)}) %collective-permute-start.24) | collective-permute-done | bytes 1048608 | tf_op jit(solution)/shard_map/ppermute | solution.py:35
  133.3 1.7 fusion.70
  135.8 1.7 fusion.67
  137.5 9.6 %collective-permute-done.26 = bf16[1024,512]{1,0:T(8,128)(2,1)} collective-permute-done((bf16[1024,512]{1,0:T(8,128)(2,1)S(1)}, bf16[1024,512]{1,0:T(8,128)(2,1)}, u32[]{:S(2)}, u32[]{:S(2)}) %collective-permute-start.26) | collective-permute-done | bytes 1048608 | tf_op jit(solution)/shard_map/ppermute | solution.py:35
  147.1 1.8 fusion.64
  150.4 12.7 %collective-permute-start.27 = (bf16[384,512]{1,0:T(8,128)(2,1)S(1)}, bf16[384,512]{1,0:T(8,128)(2,1)S(1)}, u32[]{:S(2)}, u32[]{:S(2)}) collective-permute-start(bf16[384,512]{1,0:T(8,128)(2,1)S(1)} %fusion.15), channel_id=1, source_target_pairs={{0,1},{1,0},{2,3},{3,2},{4,5},{5,4},{6,7},{7,6},{8,9},{9,8},{10,11... | collective-permute-start | bytes 1179656 | tf_op jit(solution)/shard_map/ppermute | solution.py:35
  163.1 1.8 collective-permute-start.28
  165.0 1.3 constant_dynamic-update-slice_fusion.26
  166.3 7.3 %collective-permute-start.33 = (bf16[384,512]{1,0:T(8,128)(2,1)S(1)}, bf16[384,512]{1,0:T(8,128)(2,1)S(1)}, u32[]{:S(2)}, u32[]{:S(2)}) collective-permute-start(bf16[384,512]{1,0:T(8,128)(2,1)S(1)} %collective-permute-done.32), channel_id=1, source_target_pairs={{0,1},{1,0},{2,3},{3,2},{4,5},{5,4},{6,7},{7,6},{8,9},{9,8},{10,11... | collective-permute-start | bytes 1179656 | tf_op jit(solution)/shard_map/ppermute | solution.py:35
  173.7 2.5 collective-permute-done.28
  176.2 1.4 collective-permute-start.29
  177.6 1.4 collective-permute-done.30
  184.8 8.3 %collective-permute-done.35 = bf16[384,512]{1,0:T(8,128)(2,1)S(1)} collective-permute-done((bf16[384,512]{1,0:T(8,128)(2,1)S(1)}, bf16[384,512]{1,0:T(8,128)(2,1)S(1)}, u32[]{:S(2)}, u32[]{:S(2)}) %collective-permute-start.35) | collective-permute-done | bytes 393248 | tf_op jit(solution)/shard_map/ppermute | solution.py:35
  194.6 2.6 collective-permute-start.38
  197.2 6.8 %collective-permute-done.39 = bf16[384,512]{1,0:T(8,128)(2,1)S(1)} collective-permute-done((bf16[384,512]{1,0:T(8,128)(2,1)S(1)}, bf16[384,512]{1,0:T(8,128)(2,1)S(1)}, u32[]{:S(2)}, u32[]{:S(2)}) %collective-permute-start.39) | collective-permute-done | bytes 393248 | tf_op jit(solution)/shard_map/ppermute | solution.py:35
  208.1 1.8 collective-permute-start.41
  212.5 22.1 %collective-permute-done.41 = bf16[1024,512]{1,0:T(8,128)(2,1)S(1)} collective-permute-done((bf16[1024,512]{1,0:T(8,128)(2,1)S(1)}, bf16[1024,512]{1,0:T(8,128)(2,1)S(1)}, u32[]{:S(2)}, u32[]{:S(2)}) %collective-permute-start.41) | collective-permute-done | bytes 1048608 | tf_op jit(solution)/shard_map/ppermute | solution.py:35
  235.4 2.7 collective-permute-start.45
  238.0 4.0 %collective-permute-done.44 = bf16[256,512]{1,0:T(8,128)(2,1)S(1)} collective-permute-done((bf16[256,512]{1,0:T(8,128)(2,1)S(1)}, bf16[256,512]{1,0:T(8,128)(2,1)S(1)}, u32[]{:S(2)}, u32[]{:S(2)}) %collective-permute-start.44) | collective-permute-done | bytes 262176 | tf_op jit(solution)/shard_map/ppermute | solution.py:35
  242.1 2.1 collective-permute-done.45
  245.3 2.6 collective-permute-start.47
  248.5 5.5 %collective-permute-done.47 = bf16[256,512]{1,0:T(8,128)(2,1)S(1)} collective-permute-done((bf16[256,512]{1,0:T(8,128)(2,1)S(1)}, bf16[256,512]{1,0:T(8,128)(2,1)S(1)}, u32[]{:S(2)}, u32[]{:S(2)}) %collective-permute-start.47) | collective-permute-done | bytes 262176 | tf_op jit(solution)/shard_map/ppermute | solution.py:35
  254.7 2.7 collective-permute-done.49
  257.4 2.6 collective-permute-start.50
  260.1 1.3 collective-permute-start.52
  261.3 21.7 %collective-permute-done.50 = bf16[1024,512]{1,0:T(8,128)(2,1)S(1)} collective-permute-done((bf16[1024,512]{1,0:T(8,128)(2,1)S(1)}, bf16[1024,512]{1,0:T(8,128)(2,1)S(1)}, u32[]{:S(2)}, u32[]{:S(2)}) %collective-permute-start.50) | collective-permute-done | bytes 1048608 | tf_op jit(solution)/shard_map/ppermute | solution.py:35
  283.6 2.8 collective-permute-done.51
  289.4 5.7 %collective-permute-start.53 = (bf16[384,512]{1,0:T(8,128)(2,1)S(1)}, bf16[384,512]{1,0:T(8,128)(2,1)S(1)}, u32[]{:S(2)}, u32[]{:S(2)}) collective-permute-start(bf16[384,512]{1,0:T(8,128)(2,1)S(1)} %fusion.13), channel_id=1, source_target_pairs={{0,1},{1,0},{2,3},{3,2},{4,5},{5,4},{6,7},{7,6},{8,9},{9,8},{10,11... | collective-permute-start | bytes 1179656 | tf_op jit(solution)/shard_map/ppermute | solution.py:35
  296.8 8.4 %collective-permute-start.59 = (bf16[384,512]{1,0:T(8,128)(2,1)S(1)}, bf16[384,512]{1,0:T(8,128)(2,1)S(1)}, u32[]{:S(2)}, u32[]{:S(2)}) collective-permute-start(bf16[384,512]{1,0:T(8,128)(2,1)S(1)} %collective-permute-done.58), channel_id=1, source_target_pairs={{0,1},{1,0},{2,3},{3,2},{4,5},{5,4},{6,7},{7,6},{8,9},{9,8},{10,11... | collective-permute-start | bytes 1179656 | tf_op jit(solution)/shard_map/ppermute | solution.py:35
  305.4 2.8 collective-permute-done.54
  308.2 1.5 collective-permute-start.55
  314.0 12.6 %all_to_all.5 = bf16[16,16,2,384]{3,1,2,0:T(8,128)(2,1)S(1)} all-to-all(bf16[16,16,2,384]{3,1,2,0:T(8,128)(2,1)S(1)} %copy.9), channel_id=1, replica_groups=mesh['xlo'=2,'z'=4,'y'=4,'xhi'=2,'core'=2] {'y','xhi','core'}, dimensions={0} | all-to-all | bytes 786432 | tf_op jit(solution)/shard_map/all_to_all | solution.py:152
  (145 shorter events, 50.1 us)
Async XLA Ops:
  0.9 7.8 %collective-permute-start.7 = (bf16[384,256]{1,0:T(8,128)(2,1)S(1)}, bf16[384,256]{1,0:T(8,128)(2,1)S(1)}, u32[]{:S(2)}, u32[]{:S(2)}) collective-permute-start(bf16[384,256]{1,0:T(8,128)(2,1)S(1)} %constant_dynamic-slice_fusion), channel_id=1, source_target_pairs={{0,2},{1,3},{2,0},{3,1},{4,6},{5,7},{6,4},{7,5},{8,10},{9,11},{10,... | collective-permute-start | bytes 589832 | tf_op jit(solution)/shard_map/ppermute | solution.py:35
  8.7 1.1 copy-start.3
  11.7 11.5 %collective-permute-start.9 = (bf16[384,512]{1,0:T(8,128)(2,1)}, bf16[384,512]{1,0:T(8,128)(2,1)}, u32[]{:S(2)}, u32[]{:S(2)}) collective-permute-start(bf16[384,512]{1,0:T(8,128)(2,1)} %pad_maximum_fusion), channel_id=1, source_target_pairs={{0,12},{1,13},{2,14},{3,15},{4,0},{5,1},{6,2},{7,3},{8,4},{9,5},{1... | collective-permute-start | bytes 1179656 | tf_op jit(solution)/shard_map/ppermute | solution.py:35
  14.8 18.1 %collective-permute-start.11 = (bf16[384,512]{1,0:T(8,128)(2,1)}, bf16[384,512]{1,0:T(8,128)(2,1)}, u32[]{:S(2)}, u32[]{:S(2)}) collective-permute-start(bf16[384,512]{1,0:T(8,128)(2,1)} %pad_maximum_fusion), channel_id=1, source_target_pairs={{0,8},{1,9},{2,10},{3,11},{4,12},{5,13},{6,14},{7,15},{8,0},{9,1},... | collective-permute-start | bytes 1179656 | tf_op jit(solution)/shard_map/ppermute | solution.py:35
  15.1 20.9 %collective-permute-start.13 = (bf16[384,512]{1,0:T(8,128)(2,1)}, bf16[384,512]{1,0:T(8,128)(2,1)}, u32[]{:S(2)}, u32[]{:S(2)}) collective-permute-start(bf16[384,512]{1,0:T(8,128)(2,1)} %pad_maximum_fusion), channel_id=1, source_target_pairs={{0,4},{1,5},{2,6},{3,7},{4,8},{5,9},{6,10},{7,11},{8,12},{9,13},{1... | collective-permute-start | bytes 1179656 | tf_op jit(solution)/shard_map/ppermute | solution.py:35
  15.8 20.7 %collective-permute-start.8 = (bf16[384,512]{1,0:T(8,128)(2,1)}, bf16[384,512]{1,0:T(8,128)(2,1)}, u32[]{:S(2)}, u32[]{:S(2)}) collective-permute-start(bf16[384,512]{1,0:T(8,128)(2,1)} %pad_maximum_fusion), channel_id=1, source_target_pairs={{0,1},{1,0},{2,3},{3,2},{4,5},{5,4},{6,7},{7,6},{8,9},{9,8},{10,11... | collective-permute-start | bytes 1179656 | tf_op jit(solution)/shard_map/ppermute | solution.py:35
  23.1 15.5 %collective-permute-start.10 = (bf16[384,512]{1,0:T(8,128)(2,1)}, bf16[384,512]{1,0:T(8,128)(2,1)}, u32[]{:S(2)}, u32[]{:S(2)}) collective-permute-start(bf16[384,512]{1,0:T(8,128)(2,1)} %collective-permute-done.9), channel_id=1, source_target_pairs={{0,1},{1,0},{2,3},{3,2},{4,5},{5,4},{6,7},{7,6},{8,9},{9,8},{10,11... | collective-permute-start | bytes 1179656 | tf_op jit(solution)/shard_map/ppermute | solution.py:35
  32.9 7.9 %collective-permute-start.12 = (bf16[384,512]{1,0:T(8,128)(2,1)}, bf16[384,512]{1,0:T(8,128)(2,1)S(1)}, u32[]{:S(2)}, u32[]{:S(2)}) collective-permute-start(bf16[384,512]{1,0:T(8,128)(2,1)} %collective-permute-done.11), channel_id=1, source_target_pairs={{0,1},{1,0},{2,3},{3,2},{4,5},{5,4},{6,7},{7,6},{8,9},{9,8},{10,11... | collective-permute-start | bytes 1179656 | tf_op jit(solution)/shard_map/ppermute | solution.py:35
  36.1 5.8 %collective-permute-start.14 = (bf16[384,512]{1,0:T(8,128)(2,1)}, bf16[384,512]{1,0:T(8,128)(2,1)S(1)}, u32[]{:S(2)}, u32[]{:S(2)}) collective-permute-start(bf16[384,512]{1,0:T(8,128)(2,1)} %collective-permute-done.13), channel_id=1, source_target_pairs={{0,1},{1,0},{2,3},{3,2},{4,5},{5,4},{6,7},{7,6},{8,9},{9,8},{10,11... | collective-permute-start | bytes 1179656 | tf_op jit(solution)/shard_map/ppermute | solution.py:35
  41.9 10.5 %copy-start = (bf16[384,4096]{1,0:T(8,128)(2,1)}, bf16[384,4096]{1,0:T(8,128)(2,1)S(1)}, u32[]{:S(2)}) copy-start(bf16[384,4096]{1,0:T(8,128)(2,1)S(1)} %constant_dynamic-update-slice_fusion) | copy-start | bytes 9437188
  43.9 16.3 %collective-permute-start.15 = (bf16[1024,512]{1,0:T(8,128)(2,1)}, bf16[1024,512]{1,0:T(8,128)(2,1)}, u32[]{:S(2)}, u32[]{:S(2)}) collective-permute-start(bf16[1024,512]{1,0:T(8,128)(2,1)} %convolution_convert_fusion.5), channel_id=1, source_target_pairs={{0,64},{1,17},{2,66},{3,19},{4,68},{5,21},{6,70},{7,23},{8,72},{9,... | collective-permute-start | bytes 3145736 | tf_op jit(solution)/shard_map/ppermute | solution.py:35
  47.3 25.4 %collective-permute-start.16 = (bf16[1024,512]{1,0:T(8,128)(2,1)}, bf16[1024,512]{1,0:T(8,128)(2,1)}, u32[]{:S(2)}, u32[]{:S(2)}) collective-permute-start(bf16[1024,512]{1,0:T(8,128)(2,1)} %convolution_convert_fusion.4), channel_id=1, source_target_pairs={{0,66},{1,49},{2,64},{3,51},{4,70},{5,53},{6,68},{7,55},{8,74},{9,... | collective-permute-start | bytes 3145736 | tf_op jit(solution)/shard_map/ppermute | solution.py:35
  51.2 21.6 %collective-permute-start.17 = (bf16[1024,512]{1,0:T(8,128)(2,1)}, bf16[1024,512]{1,0:T(8,128)(2,1)}, u32[]{:S(2)}, u32[]{:S(2)}) collective-permute-start(bf16[1024,512]{1,0:T(8,128)(2,1)} %convolution_convert_fusion.3), channel_id=1, source_target_pairs={{0,2},{1,33},{2,0},{3,35},{4,6},{5,37},{6,4},{7,39},{8,10},{9,41},... | collective-permute-start | bytes 3145736 | tf_op jit(solution)/shard_map/ppermute | solution.py:35
  53.2 26.4 %copy-start.2 = (bf16[768,256]{1,0:T(8,128)(2,1)S(1)}, bf16[768,256]{1,0:T(8,128)(2,1)}, u32[]{:S(2)}) copy-start(bf16[768,256]{1,0:T(8,128)(2,1)} %param.1) | copy-start | bytes 1179652
  75.4 29.2 %collective-permute-start.18 = (bf16[256,512]{1,0:T(8,128)(2,1)S(1)}, bf16[256,512]{1,0:T(8,128)(2,1)S(1)}, u32[]{:S(2)}, u32[]{:S(2)}) collective-permute-start(bf16[256,512]{1,0:T(8,128)(2,1)S(1)} %get-tuple-element.16), channel_id=1, source_target_pairs={{0,16},{1,65},{2,18},{3,67},{4,20},{5,69},{6,22},{7,71},{8,24},{9,... | collective-permute-start | bytes 786440 | tf_op jit(solution)/shard_map/ppermute | solution.py:35
  76.7 27.9 %collective-permute-start.19 = (bf16[256,512]{1,0:T(8,128)(2,1)S(1)}, bf16[256,512]{1,0:T(8,128)(2,1)}, u32[]{:S(2)}, u32[]{:S(2)}) collective-permute-start(bf16[256,512]{1,0:T(8,128)(2,1)S(1)} %get-tuple-element.18), channel_id=1, source_target_pairs={{0,48},{1,67},{2,50},{3,65},{4,52},{5,71},{6,54},{7,69},{8,56},{9,... | collective-permute-start | bytes 786440 | tf_op jit(solution)/shard_map/ppermute | solution.py:35
  78.2 27.1 %collective-permute-start.20 = (bf16[256,512]{1,0:T(8,128)(2,1)S(1)}, bf16[256,512]{1,0:T(8,128)(2,1)}, u32[]{:S(2)}, u32[]{:S(2)}) collective-permute-start(bf16[256,512]{1,0:T(8,128)(2,1)S(1)} %get-tuple-element.17), channel_id=1, source_target_pairs={{0,32},{1,3},{2,34},{3,1},{4,36},{5,7},{6,38},{7,5},{8,40},{9,11},... | collective-permute-start | bytes 786440 | tf_op jit(solution)/shard_map/ppermute | solution.py:35
  79.8 2.7 collective-permute-start
  82.6 2.9 collective-permute-start.1
  85.4 4.0 %collective-permute-start.2 = (f32[8,128]{1,0:T(8,128)S(1)}, f32[8,128]{1,0:T(8,128)S(1)}, u32[]{:S(2)}, u32[]{:S(2)}) collective-permute-start(f32[8,128]{1,0:T(8,128)S(1)} %add.242), channel_id=1, source_target_pairs={{0,8},{1,9},{2,10},{3,11},{4,12},{5,13},{6,14},{7,15},{8,0},{9,1},... | collective-permute-start | bytes 12296 | tf_op jit(solution)/shard_map/ppermute | solution.py:35
  89.4 3.5 %collective-permute-start.3 = (f32[8,128]{1,0:T(8,128)S(1)}, f32[8,128]{1,0:T(8,128)S(1)}, u32[]{:S(2)}, u32[]{:S(2)}) collective-permute-start(f32[8,128]{1,0:T(8,128)S(1)} %add.243), channel_id=1, source_target_pairs={{0,64},{1,65},{2,66},{3,67},{4,68},{5,69},{6,70},{7,71},{8,72},{9,... | collective-permute-start | bytes 12296 | tf_op jit(solution)/shard_map/ppermute | solution.py:35
  92.9 4.0 %collective-permute-start.4 = (f32[8,128]{1,0:T(8,128)S(1)}, f32[8,128]{1,0:T(8,128)S(1)}, u32[]{:S(2)}, u32[]{:S(2)}) collective-permute-start(f32[8,128]{1,0:T(8,128)S(1)} %add.244), channel_id=1, source_target_pairs={{0,2},{1,3},{2,0},{3,1},{4,6},{5,7},{6,4},{7,5},{8,10},{9,11},{10,... | collective-permute-start | bytes 12296 | tf_op jit(solution)/shard_map/ppermute | solution.py:35
  96.8 2.5 collective-permute-start.5
  99.3 4.0 %collective-permute-start.6 = (f32[8,128]{1,0:T(8,128)S(1)}, f32[8,128]{1,0:T(8,128)S(1)}, u32[]{:S(2)}, u32[]{:S(2)}) collective-permute-start(f32[8,128]{1,0:T(8,128)S(1)} %add.246), channel_id=1, source_target_pairs={{0,32},{1,33},{2,34},{3,35},{4,36},{5,37},{6,38},{7,39},{8,40},{9,... | collective-permute-start | bytes 12296 | tf_op jit(solution)/shard_map/ppermute | solution.py:35
  106.7 8.6 %collective-permute-start.21 = (bf16[256,512]{1,0:T(8,128)(2,1)S(1)}, bf16[256,512]{1,0:T(8,128)(2,1)S(1)}, u32[]{:S(2)}, u32[]{:S(2)}) collective-permute-start(bf16[256,512]{1,0:T(8,128)(2,1)S(1)} %get-tuple-element.8), channel_id=1, source_target_pairs={{0,48},{1,67},{2,50},{3,65},{4,52},{5,71},{6,54},{7,69},{8,56},{9,... | collective-permute-start | bytes 786440 | tf_op jit(solution)/shard_map/ppermute | solution.py:35
  109.1 6.8 %collective-permute-start.22 = (bf16[256,512]{1,0:T(8,128)(2,1)S(1)}, bf16[256,512]{1,0:T(8,128)(2,1)S(1)}, u32[]{:S(2)}, u32[]{:S(2)}) collective-permute-start(bf16[256,512]{1,0:T(8,128)(2,1)S(1)} %get-tuple-element.8), channel_id=1, source_target_pairs={{0,32},{1,3},{2,34},{3,1},{4,36},{5,7},{6,38},{7,5},{8,40},{9,11},... | collective-permute-start | bytes 786440 | tf_op jit(solution)/shard_map/ppermute | solution.py:35
  110.0 9.0 %collective-permute-start.23 = (bf16[256,512]{1,0:T(8,128)(2,1)S(1)}, bf16[256,512]{1,0:T(8,128)(2,1)S(1)}, u32[]{:S(2)}, u32[]{:S(2)}) collective-permute-start(bf16[256,512]{1,0:T(8,128)(2,1)S(1)} %get-tuple-element.8), channel_id=1, source_target_pairs={{0,16},{1,65},{2,18},{3,67},{4,20},{5,69},{6,22},{7,71},{8,24},{9,... | collective-permute-start | bytes 786440 | tf_op jit(solution)/shard_map/ppermute | solution.py:35
  119.0 14.3 %collective-permute-start.24 = (bf16[1024,512]{1,0:T(8,128)(2,1)S(1)}, bf16[1024,512]{1,0:T(8,128)(2,1)S(1)}, u32[]{:S(2)}, u32[]{:S(2)}) collective-permute-start(bf16[1024,512]{1,0:T(8,128)(2,1)S(1)} %constant_dynamic-update-slice_fusion.29), channel_id=1, source_target_pairs={{0,66},{1,49},{2,64},{3,51},{4,70},{5,53},{6,68},{7,55},{8,74},{9,... | collective-permute-start | bytes 3145736 | tf_op jit(solution)/shard_map/ppermute | solution.py:35
  119.5 16.3 %collective-permute-start.25 = (bf16[1024,512]{1,0:T(8,128)(2,1)S(1)}, bf16[1024,512]{1,0:T(8,128)(2,1)S(1)}, u32[]{:S(2)}, u32[]{:S(2)}) collective-permute-start(bf16[1024,512]{1,0:T(8,128)(2,1)S(1)} %constant_dynamic-update-slice_fusion.29), channel_id=1, source_target_pairs={{0,64},{1,17},{2,66},{3,19},{4,68},{5,21},{6,70},{7,23},{8,72},{9,... | collective-permute-start | bytes 3145736 | tf_op jit(solution)/shard_map/ppermute | solution.py:35
  120.5 26.6 %collective-permute-start.26 = (bf16[1024,512]{1,0:T(8,128)(2,1)S(1)}, bf16[1024,512]{1,0:T(8,128)(2,1)}, u32[]{:S(2)}, u32[]{:S(2)}) collective-permute-start(bf16[1024,512]{1,0:T(8,128)(2,1)S(1)} %constant_dynamic-update-slice_fusion.29), channel_id=1, source_target_pairs={{0,2},{1,33},{2,0},{3,35},{4,6},{5,37},{6,4},{7,39},{8,10},{9,41},... | collective-permute-start | bytes 3145736 | tf_op jit(solution)/shard_map/ppermute | solution.py:35
  121.7 25.4 %copy-start.1 = (bf16[384,4096]{1,0:T(8,128)(2,1)S(1)}, bf16[384,4096]{1,0:T(8,128)(2,1)}, u32[]{:S(2)}) copy-start(bf16[384,4096]{1,0:T(8,128)(2,1)} %copy-done) | copy-start | bytes 9437188
  149.5 16.8 %collective-permute-start.32 = (bf16[384,512]{1,0:T(8,128)(2,1)S(1)}, bf16[384,512]{1,0:T(8,128)(2,1)S(1)}, u32[]{:S(2)}, u32[]{:S(2)}) collective-permute-start(bf16[384,512]{1,0:T(8,128)(2,1)S(1)} %fusion.15), channel_id=1, source_target_pairs={{0,8},{1,9},{2,10},{3,11},{4,12},{5,13},{6,14},{7,15},{8,0},{9,1},... | collective-permute-start | bytes 1179656 | tf_op jit(solution)/shard_map/ppermute | solution.py:35
  150.4 29.5 %collective-permute-start.27 = (bf16[384,512]{1,0:T(8,128)(2,1)S(1)}, bf16[384,512]{1,0:T(8,128)(2,1)S(1)}, u32[]{:S(2)}, u32[]{:S(2)}) collective-permute-start(bf16[384,512]{1,0:T(8,128)(2,1)S(1)} %fusion.15), channel_id=1, source_target_pairs={{0,1},{1,0},{2,3},{3,2},{4,5},{5,4},{6,7},{7,6},{8,9},{9,8},{10,11... | collective-permute-start | bytes 1179656 | tf_op jit(solution)/shard_map/ppermute | solution.py:35
  163.1 13.1 %collective-permute-start.28 = (bf16[384,512]{1,0:T(8,128)(2,1)S(1)}, bf16[384,512]{1,0:T(8,128)(2,1)S(1)}, u32[]{:S(2)}, u32[]{:S(2)}) collective-permute-start(bf16[384,512]{1,0:T(8,128)(2,1)S(1)} %fusion.15), channel_id=1, source_target_pairs={{0,12},{1,13},{2,14},{3,15},{4,0},{5,1},{6,2},{7,3},{8,4},{9,5},{1... | collective-permute-start | bytes 1179656 | tf_op jit(solution)/shard_map/ppermute | solution.py:35
  164.8 14.2 %collective-permute-start.30 = (bf16[384,512]{1,0:T(8,128)(2,1)S(1)}, bf16[384,512]{1,0:T(8,128)(2,1)S(1)}, u32[]{:S(2)}, u32[]{:S(2)}) collective-permute-start(bf16[384,512]{1,0:T(8,128)(2,1)S(1)} %fusion.15), channel_id=1, source_target_pairs={{0,4},{1,5},{2,6},{3,7},{4,8},{5,9},{6,10},{7,11},{8,12},{9,13},{1... | collective-permute-start | bytes 1179656 | tf_op jit(solution)/shard_map/ppermute | solution.py:35
  166.3 14.1 %collective-permute-start.33 = (bf16[384,512]{1,0:T(8,128)(2,1)S(1)}, bf16[384,512]{1,0:T(8,128)(2,1)S(1)}, u32[]{:S(2)}, u32[]{:S(2)}) collective-permute-start(bf16[384,512]{1,0:T(8,128)(2,1)S(1)} %collective-permute-done.32), channel_id=1, source_target_pairs={{0,1},{1,0},{2,3},{3,2},{4,5},{5,4},{6,7},{7,6},{8,9},{9,8},{10,11... | collective-permute-start | bytes 1179656 | tf_op jit(solution)/shard_map/ppermute | solution.py:35
  176.2 4.8 %collective-permute-start.29 = (bf16[384,512]{1,0:T(8,128)(2,1)S(1)}, bf16[384,512]{1,0:T(8,128)(2,1)S(1)}, u32[]{:S(2)}, u32[]{:S(2)}) collective-permute-start(bf16[384,512]{1,0:T(8,128)(2,1)S(1)} %collective-permute-done.28), channel_id=1, source_target_pairs={{0,1},{1,0},{2,3},{3,2},{4,5},{5,4},{6,7},{7,6},{8,9},{9,8},{10,11... | collective-permute-start | bytes 1179656 | tf_op jit(solution)/shard_map/ppermute | solution.py:35
  179.1 2.5 collective-permute-start.31
  182.3 10.8 %collective-permute-start.35 = (bf16[384,512]{1,0:T(8,128)(2,1)S(1)}, bf16[384,512]{1,0:T(8,128)(2,1)S(1)}, u32[]{:S(2)}, u32[]{:S(2)}) collective-permute-start(bf16[384,512]{1,0:T(8,128)(2,1)S(1)} %get-tuple-element.20), channel_id=1, source_target_pairs={{0,12},{1,13},{2,14},{3,15},{4,0},{5,1},{6,2},{7,3},{8,4},{9,5},{1... | collective-permute-start | bytes 1179656 | tf_op jit(solution)/shard_map/ppermute | solution.py:35
  183.0 11.6 %collective-permute-start.37 = (bf16[384,512]{1,0:T(8,128)(2,1)S(1)}, bf16[384,512]{1,0:T(8,128)(2,1)S(1)}, u32[]{:S(2)}, u32[]{:S(2)}) collective-permute-start(bf16[384,512]{1,0:T(8,128)(2,1)S(1)} %get-tuple-element.20), channel_id=1, source_target_pairs={{0,8},{1,9},{2,10},{3,11},{4,12},{5,13},{6,14},{7,15},{8,0},{9,1},... | collective-permute-start | bytes 1179656 | tf_op jit(solution)/shard_map/ppermute | solution.py:35
  183.9 20.1 %collective-permute-start.39 = (bf16[384,512]{1,0:T(8,128)(2,1)S(1)}, bf16[384,512]{1,0:T(8,128)(2,1)S(1)}, u32[]{:S(2)}, u32[]{:S(2)}) collective-permute-start(bf16[384,512]{1,0:T(8,128)(2,1)S(1)} %get-tuple-element.20), channel_id=1, source_target_pairs={{0,4},{1,5},{2,6},{3,7},{4,8},{5,9},{6,10},{7,11},{8,12},{9,13},{1... | collective-permute-start | bytes 1179656 | tf_op jit(solution)/shard_map/ppermute | solution.py:35
  183.9 20.6 %collective-permute-start.34 = (bf16[384,512]{1,0:T(8,128)(2,1)S(1)}, bf16[384,512]{1,0:T(8,128)(2,1)S(1)}, u32[]{:S(2)}, u32[]{:S(2)}) collective-permute-start(bf16[384,512]{1,0:T(8,128)(2,1)S(1)} %get-tuple-element.20), channel_id=1, source_target_pairs={{0,1},{1,0},{2,3},{3,2},{4,5},{5,4},{6,7},{7,6},{8,9},{9,8},{10,11... | collective-permute-start | bytes 1179656 | tf_op jit(solution)/shard_map/ppermute | solution.py:35
  193.1 11.5 %collective-permute-start.36 = (bf16[384,512]{1,0:T(8,128)(2,1)S(1)}, bf16[384,512]{1,0:T(8,128)(2,1)S(1)}, u32[]{:S(2)}, u32[]{:S(2)}) collective-permute-start(bf16[384,512]{1,0:T(8,128)(2,1)S(1)} %collective-permute-done.35), channel_id=1, source_target_pairs={{0,1},{1,0},{2,3},{3,2},{4,5},{5,4},{6,7},{7,6},{8,9},{9,8},{10,11... | collective-permute-start | bytes 1179656 | tf_op jit(solution)/shard_map/ppermute | solution.py:35
  194.6 10.1 %collective-permute-start.38 = (bf16[384,512]{1,0:T(8,128)(2,1)S(1)}, bf16[384,512]{1,0:T(8,128)(2,1)S(1)}, u32[]{:S(2)}, u32[]{:S(2)}) collective-permute-start(bf16[384,512]{1,0:T(8,128)(2,1)S(1)} %collective-permute-done.37), channel_id=1, source_target_pairs={{0,1},{1,0},{2,3},{3,2},{4,5},{5,4},{6,7},{7,6},{8,9},{9,8},{10,11... | collective-permute-start | bytes 1179656 | tf_op jit(solution)/shard_map/ppermute | solution.py:35
  204.0 1.8 collective-permute-start.40
  208.1 26.5 %collective-permute-start.41 = (bf16[1024,512]{1,0:T(8,128)(2,1)S(1)}, bf16[1024,512]{1,0:T(8,128)(2,1)S(1)}, u32[]{:S(2)}, u32[]{:S(2)}) collective-permute-start(bf16[1024,512]{1,0:T(8,128)(2,1)S(1)} %convolution_convert_fusion.2), channel_id=1, source_target_pairs={{0,64},{1,17},{2,66},{3,19},{4,68},{5,21},{6,70},{7,23},{8,72},{9,... | collective-permute-start | bytes 3145736 | tf_op jit(solution)/shard_map/ppermute | solution.py:35
  209.9 24.7 %collective-permute-start.42 = (bf16[1024,512]{1,0:T(8,128)(2,1)S(1)}, bf16[1024,512]{1,0:T(8,128)(2,1)S(1)}, u32[]{:S(2)}, u32[]{:S(2)}) collective-permute-start(bf16[1024,512]{1,0:T(8,128)(2,1)S(1)} %convolution_convert_fusion.1), channel_id=1, source_target_pairs={{0,66},{1,49},{2,64},{3,51},{4,70},{5,53},{6,68},{7,55},{8,74},{9,... | collective-permute-start | bytes 3145736 | tf_op jit(solution)/shard_map/ppermute | solution.py:35
  210.8 23.7 %collective-permute-start.43 = (bf16[1024,512]{1,0:T(8,128)(2,1)S(1)}, bf16[1024,512]{1,0:T(8,128)(2,1)S(1)}, u32[]{:S(2)}, u32[]{:S(2)}) collective-permute-start(bf16[1024,512]{1,0:T(8,128)(2,1)S(1)} %convolution_convert_fusion), channel_id=1, source_target_pairs={{0,2},{1,33},{2,0},{3,35},{4,6},{5,37},{6,4},{7,39},{8,10},{9,41},... | collective-permute-start | bytes 3145736 | tf_op jit(solution)/shard_map/ppermute | solution.py:35
  235.3 6.8 %collective-permute-start.44 = (bf16[256,512]{1,0:T(8,128)(2,1)S(1)}, bf16[256,512]{1,0:T(8,128)(2,1)S(1)}, u32[]{:S(2)}, u32[]{:S(2)}) collective-permute-start(bf16[256,512]{1,0:T(8,128)(2,1)S(1)} %get-tuple-element.13), channel_id=1, source_target_pairs={{0,16},{1,65},{2,18},{3,67},{4,20},{5,69},{6,22},{7,71},{8,24},{9,... | collective-permute-start | bytes 786440 | tf_op jit(solution)/shard_map/ppermute | solution.py:35
  235.4 8.8 %collective-permute-start.45 = (bf16[256,512]{1,0:T(8,128)(2,1)S(1)}, bf16[256,512]{1,0:T(8,128)(2,1)S(1)}, u32[]{:S(2)}, u32[]{:S(2)}) collective-permute-start(bf16[256,512]{1,0:T(8,128)(2,1)S(1)} %get-tuple-element.15), channel_id=1, source_target_pairs={{0,48},{1,67},{2,50},{3,65},{4,52},{5,71},{6,54},{7,69},{8,56},{9,... | collective-permute-start | bytes 786440 | tf_op jit(solution)/shard_map/ppermute | solution.py:35
  238.0 7.0 %collective-permute-start.46 = (bf16[256,512]{1,0:T(8,128)(2,1)S(1)}, bf16[256,512]{1,0:T(8,128)(2,1)S(1)}, u32[]{:S(2)}, u32[]{:S(2)}) collective-permute-start(bf16[256,512]{1,0:T(8,128)(2,1)S(1)} %get-tuple-element.14), channel_id=1, source_target_pairs={{0,32},{1,3},{2,34},{3,1},{4,36},{5,7},{6,38},{7,5},{8,40},{9,11},... | collective-permute-start | bytes 786440 | tf_op jit(solution)/shard_map/ppermute | solution.py:35
  245.3 8.7 %collective-permute-start.47 = (bf16[256,512]{1,0:T(8,128)(2,1)S(1)}, bf16[256,512]{1,0:T(8,128)(2,1)S(1)}, u32[]{:S(2)}, u32[]{:S(2)}) collective-permute-start(bf16[256,512]{1,0:T(8,128)(2,1)S(1)} %get-tuple-element.6), channel_id=1, source_target_pairs={{0,48},{1,67},{2,50},{3,65},{4,52},{5,71},{6,54},{7,69},{8,56},{9,... | collective-permute-start | bytes 786440 | tf_op jit(solution)/shard_map/ppermute | solution.py:35
  247.9 6.8 %collective-permute-start.48 = (bf16[256,512]{1,0:T(8,128)(2,1)S(1)}, bf16[256,512]{1,0:T(8,128)(2,1)S(1)}, u32[]{:S(2)}, u32[]{:S(2)}) collective-permute-start(bf16[256,512]{1,0:T(8,128)(2,1)S(1)} %get-tuple-element.6), channel_id=1, source_target_pairs={{0,32},{1,3},{2,34},{3,1},{4,36},{5,7},{6,38},{7,5},{8,40},{9,11},... | collective-permute-start | bytes 786440 | tf_op jit(solution)/shard_map/ppermute | solution.py:35
  247.9 9.5 %collective-permute-start.49 = (bf16[256,512]{1,0:T(8,128)(2,1)S(1)}, bf16[256,512]{1,0:T(8,128)(2,1)S(1)}, u32[]{:S(2)}, u32[]{:S(2)}) collective-permute-start(bf16[256,512]{1,0:T(8,128)(2,1)S(1)} %get-tuple-element.6), channel_id=1, source_target_pairs={{0,16},{1,65},{2,18},{3,67},{4,20},{5,69},{6,22},{7,71},{8,24},{9,... | collective-permute-start | bytes 786440 | tf_op jit(solution)/shard_map/ppermute | solution.py:35
  257.4 25.6 %collective-permute-start.50 = (bf16[1024,512]{1,0:T(8,128)(2,1)S(1)}, bf16[1024,512]{1,0:T(8,128)(2,1)S(1)}, u32[]{:S(2)}, u32[]{:S(2)}) collective-permute-start(bf16[1024,512]{1,0:T(8,128)(2,1)S(1)} %constant_dynamic-update-slice_fusion.21), channel_id=1, source_target_pairs={{0,66},{1,49},{2,64},{3,51},{4,70},{5,53},{6,68},{7,55},{8,74},{9,... | collective-permute-start | bytes 3145736 | tf_op jit(solution)/shard_map/ppermute | solution.py:35
  260.1 26.4 %collective-permute-start.51 = (bf16[1024,512]{1,0:T(8,128)(2,1)S(1)}, bf16[1024,512]{1,0:T(8,128)(2,1)S(1)}, u32[]{:S(2)}, u32[]{:S(2)}) collective-permute-start(bf16[1024,512]{1,0:T(8,128)(2,1)S(1)} %constant_dynamic-update-slice_fusion.21), channel_id=1, source_target_pairs={{0,64},{1,17},{2,66},{3,19},{4,68},{5,21},{6,70},{7,23},{8,72},{9,... | collective-permute-start | bytes 3145736 | tf_op jit(solution)/shard_map/ppermute | solution.py:35
  260.1 27.0 %collective-permute-start.52 = (bf16[1024,512]{1,0:T(8,128)(2,1)S(1)}, bf16[1024,512]{1,0:T(8,128)(2,1)S(1)}, u32[]{:S(2)}, u32[]{:S(2)}) collective-permute-start(bf16[1024,512]{1,0:T(8,128)(2,1)S(1)} %constant_dynamic-update-slice_fusion.21), channel_id=1, source_target_pairs={{0,2},{1,33},{2,0},{3,35},{4,6},{5,37},{6,4},{7,39},{8,10},{9,41},... | collective-permute-start | bytes 3145736 | tf_op jit(solution)/shard_map/ppermute | solution.py:35
  288.2 8.6 %collective-permute-start.58 = (bf16[384,512]{1,0:T(8,128)(2,1)S(1)}, bf16[384,512]{1,0:T(8,128)(2,1)S(1)}, u32[]{:S(2)}, u32[]{:S(2)}) collective-permute-start(bf16[384,512]{1,0:T(8,128)(2,1)S(1)} %fusion.13), channel_id=1, source_target_pairs={{0,8},{1,9},{2,10},{3,11},{4,12},{5,13},{6,14},{7,15},{8,0},{9,1},... | collective-permute-start | bytes 1179656 | tf_op jit(solution)/shard_map/ppermute | solution.py:35
  289.4 21.9 %collective-permute-start.53 = (bf16[384,512]{1,0:T(8,128)(2,1)S(1)}, bf16[384,512]{1,0:T(8,128)(2,1)S(1)}, u32[]{:S(2)}, u32[]{:S(2)}) collective-permute-start(bf16[384,512]{1,0:T(8,128)(2,1)S(1)} %fusion.13), channel_id=1, source_target_pairs={{0,1},{1,0},{2,3},{3,2},{4,5},{5,4},{6,7},{7,6},{8,9},{9,8},{10,11... | collective-permute-start | bytes 1179656 | tf_op jit(solution)/shard_map/ppermute | solution.py:35
  295.1 13.1 %collective-permute-start.54 = (bf16[384,512]{1,0:T(8,128)(2,1)S(1)}, bf16[384,512]{1,0:T(8,128)(2,1)S(1)}, u32[]{:S(2)}, u32[]{:S(2)}) collective-permute-start(bf16[384,512]{1,0:T(8,128)(2,1)S(1)} %fusion.13), channel_id=1, source_target_pairs={{0,12},{1,13},{2,14},{3,15},{4,0},{5,1},{6,2},{7,3},{8,4},{9,5},{1... | collective-permute-start | bytes 1179656 | tf_op jit(solution)/shard_map/ppermute | solution.py:35
  296.1 14.5 %collective-permute-start.56 = (bf16[384,512]{1,0:T(8,128)(2,1)S(1)}, bf16[384,512]{1,0:T(8,128)(2,1)S(1)}, u32[]{:S(2)}, u32[]{:S(2)}) collective-permute-start(bf16[384,512]{1,0:T(8,128)(2,1)S(1)} %fusion.13), channel_id=1, source_target_pairs={{0,4},{1,5},{2,6},{3,7},{4,8},{5,9},{6,10},{7,11},{8,12},{9,13},{1... | collective-permute-start | bytes 1179656 | tf_op jit(solution)/shard_map/ppermute | solution.py:35
  296.8 15.1 %collective-permute-start.59 = (bf16[384,512]{1,0:T(8,128)(2,1)S(1)}, bf16[384,512]{1,0:T(8,128)(2,1)S(1)}, u32[]{:S(2)}, u32[]{:S(2)}) collective-permute-start(bf16[384,512]{1,0:T(8,128)(2,1)S(1)} %collective-permute-done.58), channel_id=1, source_target_pairs={{0,1},{1,0},{2,3},{3,2},{4,5},{5,4},{6,7},{7,6},{8,9},{9,8},{10,11... | collective-permute-start | bytes 1179656 | tf_op jit(solution)/shard_map/ppermute | solution.py:35
  308.2 4.3 %collective-permute-start.55 = (bf16[384,512]{1,0:T(8,128)(2,1)S(1)}, bf16[384,512]{1,0:T(8,128)(2,1)S(1)}, u32[]{:S(2)}, u32[]{:S(2)}) collective-permute-start(bf16[384,512]{1,0:T(8,128)(2,1)S(1)} %collective-permute-done.54), channel_id=1, source_target_pairs={{0,1},{1,0},{2,3},{3,2},{4,5},{5,4},{6,7},{7,6},{8,9},{9,8},{10,11... | collective-permute-start | bytes 1179656 | tf_op jit(solution)/shard_map/ppermute | solution.py:35
  310.6 2.5 collective-permute-start.57
  (1 other events, 0.7 us)
